TPU v7x, 256 devices: a whole 4x4x8 slice. The times are simulated.
256 devices in a mesh: dp: 16 (over y_lo, z), tensor: 16 (over x, y_hi, core).
Axes of the slice: x: 4, y: 4 (y_hi: 2, y_lo: 2; y = y_hi * 2 + y_lo), z: 8, core: 2. Of those that a mesh axis runs over, the one named last changes fastest.
Arguments:
- tokens: bfloat16 [2048, 6144], P('dp', 'tensor'), may hold values from -6 to 6
- cotangent: bfloat16 [2048, 6144], P('dp', 'tensor'), may hold values from -6 to 6
- up_blocks: bfloat16 [96, 4, 256, 256], P('tensor'), may hold values from -0.1875 to 0.1875
- up_index: int32 [96, 4], P('tensor'), may hold values from 0 to 23, all different within a row
- down_blocks: bfloat16 [96, 4, 256, 256], P('tensor'), may hold values from -0.09375 to 0.09375
- down_index: int32 [96, 4], P('tensor'), may hold values from 0 to 23, all different within a row
Outputs:
- output: bfloat16 [2048, 6144], P('dp', 'tensor')
- input_grad: bfloat16 [2048, 6144], P('dp', 'tensor')
- up_grad: bfloat16 [96, 4, 256, 256], P('tensor', None, 'dp')
- down_grad: bfloat16 [96, 4, 256, 256], P('tensor', None, 'dp')
Inputs may be any that keep to these rules, and one draw needn't show every extreme that they name: `up_index`: each row names 4 different feature blocks; every one of the 24 feature blocks is named by some row. `down_index`: each row names 4 different feature blocks; every one of the 24 feature blocks is named by some row.
All inputs are finite; a program needn't handle non-finite values.
Results may differ from a plain program's by a relative error of at most 0.022.
Values may be sent and summed in bfloat16 or wider, within the bound.
No kernel may reach another device: no remote copies, remote signals or barrier semaphores. Data moves between devices by JAX's collectives and lax.ppermute only.
A program may use at most 64 MiB of HBM per device.

v0:
```python
import jax
import jax.numpy as jnp
from jax import lax
from jax.sharding import PartitionSpec as P

BLK = 256
DB = 24


def pick_blocks(panel, index_table):
    row_count = panel.shape[0]
    blocked = panel.reshape(row_count, DB, BLK)
    picked = jnp.take(blocked, index_table.reshape(-1), axis=1)
    return picked.reshape(row_count, index_table.shape[0], index_table.shape[1], BLK)


def place_blocks(partial_terms, index_table):
    row_count, local_blocks, fanout, block_width = partial_terms.shape
    one_hot = (index_table.reshape(-1)[:, None] == jnp.arange(DB, dtype=jnp.int32)[None, :]).astype(
        jnp.float32
    )
    placed = jnp.einsum(
        "tjd,jb->tbd",
        partial_terms.reshape(row_count, local_blocks * fanout, block_width),
        one_hot,
        precision=lax.Precision.HIGHEST,
    )
    return placed.reshape(row_count, DB * block_width)


def silu_slope(pre_act):
    sigmoid_val = jax.nn.sigmoid(pre_act)
    return sigmoid_val * (1.0 + pre_act * (1.0 - sigmoid_val))


def on_device(tokens, cotangent, up_blocks, up_index, down_blocks, down_index):
    token_panel = lax.all_gather(tokens, "tensor", axis=1, tiled=True)
    picked = pick_blocks(token_panel, up_index)
    pre_act = jnp.einsum("tnki,nkio->tno", picked, up_blocks, preferred_element_type=jnp.float32)
    hidden = jax.nn.silu(pre_act).astype(jnp.bfloat16)
    out_terms = jnp.einsum(
        "tno,nkod->tnkd", hidden, down_blocks, preferred_element_type=jnp.float32
    )
    output = lax.psum_scatter(
        place_blocks(out_terms, down_index).astype(jnp.bfloat16),
        "tensor",
        scatter_dimension=1,
        tiled=True,
    )
    grad_panel = lax.all_gather(cotangent, "tensor", axis=1, tiled=True)
    grad_picked = pick_blocks(grad_panel, down_index)
    down_local = jnp.einsum(
        "tno,tnkd->nkod", hidden, grad_picked, preferred_element_type=jnp.float32
    )
    grad_hidden = jnp.einsum(
        "tnkd,nkod->tno", grad_picked, down_blocks, preferred_element_type=jnp.float32
    )
    pre_grad = (grad_hidden * silu_slope(pre_act)).astype(jnp.bfloat16)
    in_terms = jnp.einsum("tno,nkio->tnki", pre_grad, up_blocks, preferred_element_type=jnp.float32)
    input_grad = lax.psum_scatter(
        place_blocks(in_terms, up_index).astype(jnp.bfloat16),
        "tensor",
        scatter_dimension=1,
        tiled=True,
    )
    up_local = jnp.einsum("tnki,tno->nkio", picked, pre_grad, preferred_element_type=jnp.float32)
    up_total, down_total = (
        lax.psum_scatter(
            up_local.astype(jnp.bfloat16), "dp", scatter_dimension=2, tiled=True
        ).astype(jnp.float32),
        lax.psum_scatter(
            down_local.astype(jnp.bfloat16), "dp", scatter_dimension=2, tiled=True
        ).astype(jnp.float32),
    )
    return (output, input_grad, up_total.astype(jnp.bfloat16), down_total.astype(jnp.bfloat16))


def solution(mesh):
    in_specs = (
        P("dp", "tensor"),
        P("dp", "tensor"),
        P("tensor", None, None, None),
        P("tensor", None),
        P("tensor", None, None, None),
        P("tensor", None),
    )
    out_specs = (
        P("dp", "tensor"),
        P("dp", "tensor"),
        P("tensor", None, "dp", None),
        P("tensor", None, "dp", None),
    )
    return jax.shard_map(
        on_device, mesh=mesh, in_specs=in_specs, out_specs=out_specs, check_vma=False
    )
```

profile of v0, /device:TPU:1, one launch (start us, length us, event | category | flops | bytes accessed | tf_op | source)
XLA Modules:
  0.0 528.4 jit_solution(8884686226187387333)
XLA Ops:
  7.2 0.0 all-gather.3.cloned.1.call-start
  7.2 1.8 copy.39
  9.0 0.0 all-gather.3.cloned.1.call-update
  9.0 0.0 all-gather.5.cloned.1.call-start
  9.1 1.6 copy.42
  10.8 0.0 reduce-scatter.12.cloned.1.call-start
  10.8 0.8 copy.38
  11.6 0.1 reshape.42
  11.7 0.8 copy.37
  12.4 0.1 eq.28
  12.6 54.8 %all-gather.3.cloned.1.call-done = bf16[128,6144]{0,1:T(8,128)(2,1)} async-done(((bf16[128,384]{0,1:T(8,128)(2,1)}), bf16[128,6144]{0,1:T(8,128)(2,1)}) %all-gather.3.cloned.1.call-update) | async-done | bytes 1572880 | tf_op jit(solution)/shard_map/all_gather | solution.py:37
  67.3 2.6 copy.40
  69.9 51.3 %all-gather.5.cloned.1.call-done = bf16[128,6144]{0,1:T(8,128)(2,1)} async-done(((bf16[128,384]{0,1:T(8,128)(2,1)}), bf16[128,6144]{0,1:T(8,128)(2,1)}) %all-gather.5.cloned.1.call-update) | async-done | bytes 1572880 | tf_op jit(solution)/shard_map/all_gather | solution.py:50
  121.2 2.6 copy.43
  123.9 3.3 gather_fusion
  127.1 1.6 broadcast_select_fusion.1
  128.7 1.1 copy-done.1
  129.9 1.5 convolution_bitcast_fusion.1
  131.4 3.3 gather_fusion.1
  134.6 1.7 broadcast_select_fusion
  136.3 1.1 copy-done.3
  137.5 3.1 fusion.18
  140.6 1.1 fusion.28
  141.7 4.5 fusion.10
  146.3 2.8 copy.60
  149.1 0.0 reduce-scatter.12.cloned.1.call-update
  149.1 0.2 reduce-scatter.10.cloned.1.call-start
  149.4 2.8 fusion.20
  152.2 4.5 fusion.13
  156.7 2.8 copy.59
  159.6 0.0 reduce-scatter.10.cloned.1.call-update
  159.6 0.0 all-reduce.3.cloned.1.call-start
  159.6 4.4 convert_bitcast_fusion
  164.0 6.3 %copy.47 = bf16[6,4,256,256]{3,1,0,2:T(4,128)(2,1)} copy(bf16[6,4,256,256]{2,3,1,0:T(8,128)(2,1)} %convert_bitcast_fusion) | data formatting | bytes 6291456 | tf_op jit(solution)/shard_map/convert_element_type | solution.py:72
  170.3 0.0 all-reduce.3.cloned.1.call-update
  170.3 0.0 reduce-scatter.8.cloned.1.call-start
  170.4 4.2 convolution_convert_fusion
  174.6 0.0 reduce-scatter.8.cloned.1.call-update
  174.6 0.6 copy-done.4
  175.3 0.6 dynamic-slice
  176.5 45.8 %reduce-scatter.12.cloned.1.call-done = bf16[384,128]{1,0:T(8,128)(2,1)} async-done(((bf16[6144,128]{1,0:T(8,128)(2,1)}), bf16[384,128]{1,0:T(8,128)(2,1)}) %reduce-scatter.12.cloned.1.call-update) | async-done | bytes 98320
  222.3 1.6 copy.58
  223.9 78.0 %reduce-scatter.10.cloned.1.call-done = bf16[384,128]{1,0:T(8,128)(2,1)} async-done(((bf16[6144,128]{1,0:T(8,128)(2,1)}), bf16[384,128]{1,0:T(8,128)(2,1)}) %reduce-scatter.10.cloned.1.call-update) | async-done | bytes 98320
  302.0 1.6 copy.56
  303.6 140.1 %all-reduce.3.cloned.1.call-done = bf16[6,4,256,256]{3,1,0,2:T(4,128)(2,1)} async-done(((bf16[6,4,256,256]{3,1,0,2:T(4,128)(2,1)}), bf16[6,4,256,256]{3,1,0,2:T(4,128)(2,1)}) %all-reduce.3.cloned.1.call-update) | async-done | bytes 3145744
  443.8 1.0 constant_dynamic-slice_fusion
  444.8 0.7 copy.48
  445.5 76.0 %reduce-scatter.8.cloned.1.call-done = bf16[6,4,16,256]{3,2,1,0:T(8,128)(2,1)} async-done(((bf16[6,4,256,256]{3,2,1,0:T(8,128)(2,1)}), bf16[6,4,16,256]{3,2,1,0:T(8,128)(2,1)}) %reduce-scatter.8.cloned.1.call-update) | async-done | bytes 196624 | tf_op jit(solution)/shard_map/reduce_scatter | solution.py:68
  (14 shorter events, 0.1 us)
Async XLA Ops:
  7.2 122.7 %copy-start = (bf16[6,4,256,256]{3,2,1,0:T(8,128)(2,1)S(1)}, bf16[6,4,256,256]{3,2,1,0:T(8,128)(2,1)}, u32[]{:S(2)}) copy-start(bf16[6,4,256,256]{3,2,1,0:T(8,128)(2,1)} %param.10) | copy-start | bytes 9437188
  7.2 60.1 %all-gather.3.cloned.1.call-start = ((), (), s32[]{:S(2)}) async-start(), calls=%async_computation.3 | async-start | bytes 1671168 | tf_op jit(solution)/shard_map/all_gather | solution.py:37
  9.0 112.2 %all-gather.5.cloned.1.call-start = ((), (), s32[]{:S(2)}) async-start(), calls=%async_computation.4 | async-start | bytes 1671168 | tf_op jit(solution)/shard_map/all_gather | solution.py:50
  10.8 211.6 %reduce-scatter.12.cloned.1.call-start = ((), (), s32[]{:S(2)}) async-start(), calls=%async_computation.7 | async-start | bytes 1671168
  128.7 1.1 copy-start.1
  134.6 2.8 copy-start.2
  136.3 1.2 copy-start.3
  149.1 152.9 %reduce-scatter.10.cloned.1.call-start = ((), (), s32[]{:S(2)}) async-start(), calls=%async_computation.6 | async-start | bytes 1671168
  159.6 284.2 %all-reduce.3.cloned.1.call-start = ((), (), s32[]{:S(2)}) async-start(), calls=%async_computation.8 | async-start | bytes 6291456
  170.3 351.2 %reduce-scatter.8.cloned.1.call-start = ((), (), s32[]{:S(2)}) async-start(), calls=%async_computation.5 | async-start | bytes 3342336 | tf_op jit(solution)/shard_map/reduce_scatter | solution.py:68
  174.6 0.7 copy-start.4
Sparse Core Ops, SparseCore 0:
  11.3 56.0 all-gather.2
  70.6 50.6 all-gather.4
  149.2 73.0 reduce-scatter.11
  226.3 75.6 reduce-scatter.9
  304.5 139.2 all-reduce.2
  446.8 74.7 reduce-scatter.7
where the time goes:
time: 537 us; the launch traced here: 528 us
  waiting for transfers between devices  446 us (83%)
  local copies, waits for them, and re-layouts  37.3 us (7%)
  matrix products  26.2 us (5%)
  between operations  14.9 us (3%)
    unnamed x9, waiting for transfers between devices  264 us
    reduce_scatter x1, waiting for transfers between devices, on_device(): lax.psum_scatter(up_local.astype(jnp.bfloat16), 'dp', scatter_dimension=2...  76 us
    all_gather x1, waiting for transfers between devices, on_device(): token_panel = lax.all_gather(tokens, 'tensor', axis=1, tiled=True)  54.8 us
    all_gather x1, waiting for transfers between devices, on_device(): grad_panel = lax.all_gather(cotangent, 'tensor', axis=1, tiled=True)  51.3 us
    unnamed x21, local copies, waits for them, and re-layouts  19.2 us
  transfers between devices with their start and end apart: 6, of which 6 were waited for; matrix products, arithmetic and copies ran while one was open for 7% of the time, Pallas kernels for 0%

commit v1 on v0

v1 whole, which is shorter than its diff:
```python
import jax
import jax.numpy as jnp
from jax import lax
from jax.experimental import pallas as pl
from jax.experimental.pallas import tpu as pltpu
from jax.sharding import Mesh, PartitionSpec as P

BLK = 256
HALF = 128
WIDE = 384
K = 4
NL = 3
AXES = ("ylo", "z", "x", "yhi", "core")
VMEM_LIMIT = 48 * 1024 * 1024


def device_id(x, y, z, c):
    return ((y % 2) * 8 + z) * 16 + x * 4 + (y // 2) * 2 + c


def permute(value, target):
    pairs = []
    for x in range(4):
        for y in range(4):
            for z in range(8):
                for c in range(2):
                    tx, ty, tc = target(x, y, c)
                    pairs.append((device_id(x, y, z, c), device_id(tx % 4, ty % 4, z, tc)))
    return lax.ppermute(value, AXES, pairs)


def other_core(x, y, c):
    return x, y, 1 - c


def other_half(x, y, c):
    return x, y ^ 1, c


def first_axis(step):
    return lambda x, y, c: (x + step, y, c) if c == 0 else (x, y + step, c)


def second_axis(step):
    return lambda x, y, c: (x, y + step, c) if c == 0 else (x + step, y, c)


def piece_tables(index_table, x, y, kind, sign):
    unit = index_table.reshape(-1)[:, None] * 2 + jnp.arange(2, dtype=jnp.int32)[None, :]
    owner = unit // 3
    lane = (unit % 3) * HALF
    px = owner // 4
    py = ((owner // 2) % 2)[:, :, None] * 2 + jnp.arange(2, dtype=jnp.int32)
    dx = ((sign * (px - x)) % 4)[:, :, None] + jnp.zeros_like(py)
    dy = (sign * (py - y)) % 4
    slot = ((owner % 2) ^ kind)[:, :, None]
    return dx, dy, slot, lane


def grads_kernel(tab_ref, tok_lane, cot_lane, tok_piece, cot_piece, *refs):
    mine, theirs = refs[0:4], refs[4:8]
    up_ref, down_ref, hid_ref, pg_ref, dw_ref = refs[8:13]
    toks, cots, ups, downs, sem = refs[13:]
    core, half = tab_ref[0], tab_ref[1]
    up_copy = pltpu.make_async_copy(up_ref.at[pl.ds(half * NL, NL)], ups, sem.at[0])
    down_copy = pltpu.make_async_copy(down_ref.at[pl.ds(half * NL, NL)], downs, sem.at[1])
    up_copy.start()

    @pl.when(core == 0)
    def _():
        for e in range(4):
            pltpu.make_async_copy(mine[e], toks.at[e], sem.at[2]).start()

    @pl.when(core == 1)
    def _():
        for e in range(4):
            pltpu.make_async_copy(theirs[e], toks.at[e], sem.at[2]).start()

    down_copy.start()

    @pl.when(core == 0)
    def _():
        for e in range(4):
            pltpu.make_async_copy(theirs[e], cots.at[e], sem.at[3]).start()

    @pl.when(core == 1)
    def _():
        for e in range(4):
            pltpu.make_async_copy(mine[e], cots.at[e], sem.at[3]).start()

    def block(ref, piece, lane, j):
        rows = []
        for h in range(2):
            cols = []
            for u in range(2):
                p = piece[(j * 2 + u) * 2 + h]
                off = pl.multiple_of(lane[j * 2 + u], HALF)
                cols.append(ref[p // 8, (p // 2) % 4, p % 2, :, pl.ds(off, HALF)])
            rows.append(jnp.concatenate(cols, axis=1))
        return jnp.concatenate(rows, axis=0)

    def store(grad, j, value):
        value = value.astype(jnp.bfloat16)
        for d in range(16):
            dw_ref[d % 8, d // 8, grad, j] = value[d * 16 : d * 16 + 16]

    up_copy.wait()
    pltpu.make_async_copy(toks, toks, sem.at[2]).wait()
    pres = []
    for n in range(NL):
        acc = jnp.zeros((BLK, BLK), jnp.float32)
        for k in range(K):
            acc += jnp.dot(
                block(toks, tok_piece, tok_lane, n * K + k),
                ups[n, k],
                preferred_element_type=jnp.float32,
            )
        pres.append(acc)
        hid_ref[n] = (acc * jax.nn.sigmoid(acc)).astype(jnp.bfloat16)
    down_copy.wait()
    pltpu.make_async_copy(cots, cots, sem.at[3]).wait()
    for n in range(NL):
        acc = jnp.zeros((BLK, BLK), jnp.float32)
        hidden = hid_ref[n]
        for k in range(K):
            cot = block(cots, cot_piece, cot_lane, n * K + k)
            acc += lax.dot_general(
                cot, downs[n, k], (((1,), (1,)), ((), ())), preferred_element_type=jnp.float32
            )
            store(
                1,
                n * K + k,
                lax.dot_general(
                    hidden, cot, (((0,), (0,)), ((), ())), preferred_element_type=jnp.float32
                ),
            )
        sig = jax.nn.sigmoid(pres[n])
        pg_ref[n] = (acc * (sig * (1.0 + pres[n] * (1.0 - sig)))).astype(jnp.bfloat16)
    for n in range(NL):
        pre_grad = pg_ref[n]
        for k in range(K):
            tok = block(toks, tok_piece, tok_lane, n * K + k)
            store(
                0,
                n * K + k,
                lax.dot_general(
                    tok, pre_grad, (((0,), (0,)), ((), ())), preferred_element_type=jnp.float32
                ),
            )


def terms_kernel(tab_ref, out_lane, in_lane, out_piece, in_piece, hid_ref, pg_ref, up_ref, down_ref, *refs):
    sends = refs[0:8]
    acc, packed, ups, downs, sem = refs[8:]
    core, half = tab_ref[0], tab_ref[1]
    up_copy = pltpu.make_async_copy(up_ref.at[pl.ds(half * NL, NL)], ups, sem.at[0])
    down_copy = pltpu.make_async_copy(down_ref.at[pl.ds(half * NL, NL)], downs, sem.at[1])
    down_copy.start()
    up_copy.start()
    acc[...] = jnp.zeros_like(acc)

    def place(kind, piece, lane, j, value):
        for h in range(2):
            for u in range(2):
                p = piece[(j * 2 + u) * 2 + h]
                off = pl.multiple_of(lane[j * 2 + u], HALF)
                acc[kind, p, :, pl.ds(off, HALF)] += value[
                    h * HALF : (h + 1) * HALF, u * HALF : (u + 1) * HALF
                ]

    down_copy.wait()
    for n in range(NL):
        for k in range(K):
            place(
                0,
                out_piece,
                out_lane,
                n * K + k,
                jnp.dot(hid_ref[n], downs[n, k], preferred_element_type=jnp.float32),
            )
    up_copy.wait()
    for n in range(NL):
        for k in range(K):
            place(
                1,
                in_piece,
                in_lane,
                n * K + k,
                lax.dot_general(
                    pg_ref[n], ups[n, k], (((1,), (1,)), ((), ())), preferred_element_type=jnp.float32
                ),
            )
    copies = []
    for d in (1, 2, 3, 0):
        for kind in range(2):
            for e in range(4):
                for s in range(2):
                    packed[kind, d, e, s] = acc[kind, (d * 4 + e) * 2 + s].astype(jnp.bfloat16)
        for side in range(2):
            kind = 1 - core if side else core
            copy = pltpu.make_async_copy(packed.at[kind, d], sends[side * 4 + d], sem.at[2 + side * 4 + d])
            copy.start()
            copies.append(copy)
    for copy in copies:
        copy.wait()


def any_spec():
    return pl.BlockSpec(memory_space=pl.ANY)


def vmem_spec():
    return pl.BlockSpec(memory_space=pltpu.VMEM)


def smem_spec():
    return pl.BlockSpec(memory_space=pltpu.SMEM)


def wide_sum(terms):
    total = terms[0].astype(jnp.float32)
    for term in terms[1:]:
        total = total + term.astype(jnp.float32)
    return total.astype(jnp.bfloat16)


def on_device(tokens, cotangent, up_blocks, up_index, down_blocks, down_index):
    x, core = lax.axis_index("x"), lax.axis_index("core")
    half = lax.axis_index("ylo")
    y = lax.axis_index("yhi") * 2 + half
    is0 = core == 0

    up_mine = lax.dynamic_slice_in_dim(up_index, half * NL, NL, 0)
    down_mine = lax.dynamic_slice_in_dim(down_index, half * NL, NL, 0)
    tab = jnp.stack([core, half]).astype(jnp.int32)
    dx, dy, slot, tok_lane = piece_tables(up_mine, x, y, 0, -1)
    tok_piece = (dy * 4 + dx) * 2 + slot
    dx, dy, slot, cot_lane = piece_tables(down_mine, x, y, 1, -1)
    cot_piece = (dx * 4 + dy) * 2 + slot
    dx, dy, slot, out_lane = piece_tables(down_mine, x, y, 0, 1)
    out_piece = (dx * 4 + dy) * 2 + slot
    dx, dy, slot, in_lane = piece_tables(up_mine, x, y, 1, 1)
    in_piece = (dy * 4 + dx) * 2 + slot
    tok_lane, tok_piece, cot_lane, cot_piece, out_lane, out_piece, in_lane, in_piece = [
        v.reshape(-1)
        for v in (tok_lane, tok_piece, cot_lane, cot_piece, out_lane, out_piece, in_lane, in_piece)
    ]

    with jax.named_scope("gather"):
        keep = jnp.where(is0, tokens, cotangent)
        give = jnp.where(is0, cotangent, tokens)
        own = jnp.stack([keep, permute(give, other_core)])
        line = [own] + [permute(own, first_axis(d)) for d in (1, 2, 3)]
        line = jnp.stack(line)
        mine = [line] + [permute(line, second_axis(e)) for e in (1, 2, 3)]
        theirs = [permute(part, other_core) for part in mine]

    bf16, f32 = jnp.bfloat16, jnp.float32
    hidden, pre_grad, weight_part = pl.pallas_call(
        grads_kernel,
        out_shape=(
            jax.ShapeDtypeStruct((NL, BLK, BLK), bf16),
            jax.ShapeDtypeStruct((NL, BLK, BLK), bf16),
            jax.ShapeDtypeStruct((8, 2, 2, NL * K, 16, BLK), bf16),
        ),
        in_specs=[smem_spec()] * 5 + [any_spec()] * 10,
        out_specs=(vmem_spec(), vmem_spec(), vmem_spec()),
        scratch_shapes=[
            pltpu.VMEM((4, 4, 2, HALF, WIDE), bf16),
            pltpu.VMEM((4, 4, 2, HALF, WIDE), bf16),
            pltpu.VMEM((NL, K, BLK, BLK), bf16),
            pltpu.VMEM((NL, K, BLK, BLK), bf16),
            pltpu.SemaphoreType.DMA((4,)),
        ],
        compiler_params=pltpu.CompilerParams(vmem_limit_bytes=VMEM_LIMIT),
        cost_estimate=pl.CostEstimate(
            flops=48 * 2 * BLK**3, bytes_accessed=13 << 20, transcendentals=NL * BLK * BLK * 2
        ),
        name="grads",
    )(tab, tok_lane, cot_lane, tok_piece, cot_piece, *mine, *theirs, up_blocks, down_blocks)

    with jax.named_scope("weight_sums"):
        weight_sum = lax.psum_scatter(
            weight_part.reshape(8 * 2 * 2 * NL * K * 16, BLK), "z", scatter_dimension=0, tiled=True
        ).reshape(2, 2, NL, K, 16, BLK)

    sends = pl.pallas_call(
        terms_kernel,
        out_shape=tuple(jax.ShapeDtypeStruct((4, 2, HALF, WIDE), bf16) for _ in range(8)),
        in_specs=[smem_spec()] * 5 + [vmem_spec()] * 2 + [any_spec()] * 2,
        out_specs=tuple(any_spec() for _ in range(8)),
        scratch_shapes=[
            pltpu.VMEM((2, 32, HALF, WIDE), f32),
            pltpu.VMEM((2, 4, 4, 2, HALF, WIDE), bf16),
            pltpu.VMEM((NL, K, BLK, BLK), bf16),
            pltpu.VMEM((NL, K, BLK, BLK), bf16),
            pltpu.SemaphoreType.DMA((10,)),
        ],
        compiler_params=pltpu.CompilerParams(vmem_limit_bytes=VMEM_LIMIT),
        cost_estimate=pl.CostEstimate(
            flops=24 * 2 * BLK**3, bytes_accessed=10 << 20, transcendentals=0
        ),
        name="terms",
    )(tab, out_lane, in_lane, out_piece, in_piece, hidden, pre_grad, up_blocks, down_blocks)

    with jax.named_scope("scatter"):
        kept, given = sends[:4], sends[4:]
        got = {d: permute(given[d], other_core) for d in (1, 2, 3, 0)}
        line = [kept[0], got[0]]
        for d in (1, 2, 3):
            line.append(permute(wide_sum([kept[d], got[d]]), first_axis(d)))
        line = wide_sum(line)
        final = [line[0]] + [permute(line[e], second_axis(e)) for e in (1, 2, 3)]
        final = wide_sum(final)
        last = permute(final[1], other_core)
        output = jnp.where(is0, final[0], last)
        input_grad = jnp.where(is0, last, final[0])

    with jax.named_scope("weight_halves"):
        stay = jnp.where(half == 0, weight_sum[0], weight_sum[1])
        leave = jnp.where(half == 0, weight_sum[1], weight_sum[0])
        come = permute(leave, other_half)
        low = jnp.where(half == 0, stay, come)
        high = jnp.where(half == 0, come, stay)
        both = jnp.concatenate([low, high], axis=1)
    return output, input_grad, both[0], both[1]


def solution(mesh):
    fine = Mesh(mesh.devices.reshape(2, 8, 4, 2, 2), AXES)
    dp, tensor = ("ylo", "z"), ("x", "yhi", "core")
    in_specs = (
        P(dp, tensor),
        P(dp, tensor),
        P(tensor, None, None, None),
        P(tensor, None),
        P(tensor, None, None, None),
        P(tensor, None),
    )
    out_specs = (
        P(dp, tensor),
        P(dp, tensor),
        P(tensor, None, dp, None),
        P(tensor, None, dp, None),
    )
    return jax.shard_map(
        on_device, mesh=fine, in_specs=in_specs, out_specs=out_specs, check_vma=False
    )
```

time: 537 us -> 119 us (0.22)
  the two profiles are of different devices: /device:TPU:1 before, /device:TPU:4 now
where the time goes in v1:
time: 119 us; the launch traced here: 118 us
  waiting for transfers between devices  59.1 us (50%)
  starting transfers between devices  22.2 us (19%)
  between operations  14.3 us (12%)
  Pallas kernels  12.1 us (10%)
  other arithmetic  6.62 us (6%)
  local copies, waits for them, and re-layouts  4.02 us (3%)
    ppermute x23, waiting for transfers between devices, permute(): return lax.ppermute(value, AXES, pairs)  53.6 us
    ppermute x23, starting transfers between devices, permute(): return lax.ppermute(value, AXES, pairs)  22.2 us
    pallas_call x1, Pallas kernels, on_device(): pl.pallas_call(grads_kernel, out_shape=(jax.ShapeDtypeStruct((NL, BLK, BL...  7 us
    reduce_scatter x1, waiting for transfers between devices, on_device(): lax.psum_scatter(weight_part.reshape(8 * 2 * 2 * NL * K * 16, BLK), 'z',...  5.49 us
    pallas_call x1, Pallas kernels, on_device(): pl.pallas_call(terms_kernel, out_shape=tuple((jax.ShapeDtypeStruct((4, 2,...  5.08 us
  transfers between devices with their start and end apart: 24, of which 14 were waited for; matrix products, arithmetic and copies ran while one was open for 6% of the time, Pallas kernels for 4%

profile of v1, /device:TPU:4, one launch (start us, length us, event | category | flops | bytes accessed | tf_op | source)
XLA Modules:
  0.0 118.3 jit_solution(11533635183345129136)
XLA Ops:
  7.2 1.0 select_bitcast_fusion
  8.3 1.3 %collective-permute-done = bf16[128,384]{1,0:T(8,128)(2,1)S(1)} collective-permute-done((bf16[128,384]{1,0:T(8,128)(2,1)S(1)}, bf16[128,384]{1,0:T(8,128)(2,1)S(1)}, u32[]{:S(2)}, u32[]{:S(2)}) %collective-permute-start) | collective-permute-done | bytes 98336 | tf_op jit(solution)/shard_map/gather/ppermute | solution.py:29
  9.6 2.3 %collective-permute-start.2 = (bf16[2,128,384]{2,1,0:T(8,128)(2,1)S(1)}, bf16[2,128,384]{2,1,0:T(8,128)(2,1)S(1)}, u32[]{:S(2)}, u32[]{:S(2)}) collective-permute-start(bf16[2,128,384]{2,1,0:T(8,128)(2,1)S(1)} %get-tuple-element.38), channel_id=1, source_target_pairs={{0,8},{1,3},{16,24},{17,19},{32,40},{33,35},{48,56},{49,51},{64,72... | collective-permute-start | bytes 589832 | tf_op jit(solution)/shard_map/gather/ppermute | solution.py:29
  12.0 0.4 collective-permute-start.1
  12.3 1.7 %collective-permute-start.3 = (bf16[2,128,384]{2,1,0:T(8,128)(2,1)S(1)}, bf16[2,128,384]{2,1,0:T(8,128)(2,1)S(1)}, u32[]{:S(2)}, u32[]{:S(2)}) collective-permute-start(bf16[2,128,384]{2,1,0:T(8,128)(2,1)S(1)} %get-tuple-element.38), channel_id=1, source_target_pairs={{0,12},{1,131},{16,28},{17,147},{32,44},{33,163},{48,60},{49,179},... | collective-permute-start | bytes 589832 | tf_op jit(solution)/shard_map/gather/ppermute | solution.py:29
  14.0 0.8 dynamic-slice_multiply_fusion
  14.9 2.1 %collective-permute-done.2 = bf16[2,128,384]{2,1,0:T(8,128)(2,1)S(1)} collective-permute-done((bf16[2,128,384]{2,1,0:T(8,128)(2,1)S(1)}, bf16[2,128,384]{2,1,0:T(8,128)(2,1)S(1)}, u32[]{:S(2)}, u32[]{:S(2)}) %collective-permute-start.2) | collective-permute-done | bytes 196640 | tf_op jit(solution)/shard_map/gather/ppermute | solution.py:29
  17.0 2.0 %collective-permute-done.1 = bf16[2,128,384]{2,1,0:T(8,128)(2,1)S(1)} collective-permute-done((bf16[2,128,384]{2,1,0:T(8,128)(2,1)S(1)}, bf16[2,128,384]{2,1,0:T(8,128)(2,1)S(1)}, u32[]{:S(2)}, u32[]{:S(2)}) %collective-permute-start.1) | collective-permute-done | bytes 196640 | tf_op jit(solution)/shard_map/gather/ppermute | solution.py:29
  19.0 0.1 pad_maximum_fusion.refs_0_
  19.1 2.2 %collective-permute-start.6 = (bf16[4,2,128,384]{3,2,1,0:T(8,128)(2,1)S(1)}, bf16[4,2,128,384]{3,2,1,0:T(8,128)(2,1)S(1)}, u32[]{:S(2)}, u32[]{:S(2)}) collective-permute-start(bf16[4,2,128,384]{3,2,1,0:T(8,128)(2,1)S(1)} %pad_maximum_fusion.refs_0_), channel_id=1, source_target_pairs={{0,130},{1,13},{16,146},{17,29},{32,162},{33,45},{48,178},{49,61},... | collective-permute-start | bytes 2359304 | tf_op jit(solution)/shard_map/gather/ppermute | solution.py:29
  21.3 0.6 collective-permute-start.5
  22.0 1.0 collective-permute-start.4
  23.2 0.1 add_select_fusion.1
  23.7 15.6 %collective-permute-done.6.refs_3_ = bf16[4,2,128,384]{3,2,1,0:T(8,128)(2,1)S(1)} collective-permute-done((bf16[4,2,128,384]{3,2,1,0:T(8,128)(2,1)S(1)}, bf16[4,2,128,384]{3,2,1,0:T(8,128)(2,1)S(1)}, u32[]{:S(2)}, u32[]{:S(2)}) %collective-permute-start.6) | collective-permute-done | bytes 786464 | tf_op jit(solution)/shard_map/gather/ppermute | solution.py:29
  39.3 0.5 collective-permute-start.9
  39.8 3.4 %collective-permute-done.4.refs_1_ = bf16[4,2,128,384]{3,2,1,0:T(8,128)(2,1)S(1)} collective-permute-done((bf16[4,2,128,384]{3,2,1,0:T(8,128)(2,1)S(1)}, bf16[4,2,128,384]{3,2,1,0:T(8,128)(2,1)S(1)}, u32[]{:S(2)}, u32[]{:S(2)}) %collective-permute-start.4) | collective-permute-done | bytes 786464 | tf_op jit(solution)/shard_map/gather/ppermute | solution.py:29
  43.4 0.1 add.464
  43.6 0.1 add.459
  44.0 0.1 add.467
  44.2 0.1 add.455
  45.2 0.5 multiply_add_fusion
  45.7 7.0 %grads.1 = (bf16[3,256,256]{2,1,0:T(8,128)(2,1)S(1)}, bf16[3,256,256]{2,1,0:T(8,128)(2,1)S(1)}, bf16[8,2,2,12,16,256]{5,4,3,2,1,0:T(8,128)(2,1)}) custom-call(s32[2]{0:T(128)S(1)} %pad_add_fusion.tab_ref, s32[24]{0:T(128)S(1)} %fusion.31.tok_lane.in_lane, s32[24]{0:T(128)S(1)} %fusion.30.cot_lane.out_lane, s32[48]{0:T(128)S(1)} %get-tuple-element.49.tok_piece, ...), custom_call_target="tpu_custom_call" | custom-call | flops 1610612736 | bytes 13631488 | tf_op jit(solution)/shard_map/grads/pallas_call | solution.py:259
  52.8 0.8 copy-done
  53.5 1.0 copy-done.1
  54.5 5.1 %terms.1 = (bf16[4,2,128,384]{3,2,1,0:T(8,128)(2,1)S(1)}, bf16[4,2,128,384]{3,2,1,0:T(8,128)(2,1)S(1)}, bf16[4,2,128,384]{3,2,1,0:T(8,128)(2,1)S(1)}, bf16[4,2,1...) custom-call(s32[2]{0:T(128)S(1)} %pad_add_fusion.tab_ref, ...), custom_call_target="tpu_custom_call" | custom-call | flops 805306368 | bytes 10485760 | tf_op jit(solution)/shard_map/terms/pallas_call | solution.py:287
  59.6 1.0 collective-permute-start.12
  60.6 0.4 collective-permute-start.16
  61.2 1.4 %collective-permute-done.12 = bf16[4,2,128,384]{3,2,1,0:T(8,128)(2,1)S(1)} collective-permute-done((bf16[4,2,128,384]{3,2,1,0:T(8,128)(2,1)S(1)}, bf16[4,2,128,384]{3,2,1,0:T(8,128)(2,1)S(1)}, u32[]{:S(2)}, u32[]{:S(2)}) %collective-permute-start.12) | collective-permute-done | bytes 786464 | tf_op jit(solution)/shard_map/scatter/ppermute | solution.py:29
  62.6 0.2 add_convert_fusion.3
  62.8 3.2 %collective-permute-start.13 = (bf16[4,2,128,384]{3,2,1,0:T(8,128)(2,1)S(1)}, bf16[4,2,128,384]{3,2,1,0:T(8,128)(2,1)S(1)}, u32[]{:S(2)}, u32[]{:S(2)}) collective-permute-start(bf16[4,2,128,384]{3,2,1,0:T(8,128)(2,1)S(1)} %add_convert_fusion.3), channel_id=1, source_target_pairs={{0,4},{1,129},{16,20},{17,145},{32,36},{33,161},{48,52},{49,177},{... | collective-permute-start | bytes 2359304 | tf_op jit(solution)/shard_map/scatter/ppermute | solution.py:29
  66.0 0.2 add_convert_fusion.2
  66.2 0.9 collective-permute-start.15
  67.1 0.2 add_convert_fusion.1
  67.3 2.7 %collective-permute-start.17 = (bf16[4,2,128,384]{3,2,1,0:T(8,128)(2,1)S(1)}, bf16[4,2,128,384]{3,2,1,0:T(8,128)(2,1)S(1)}, u32[]{:S(2)}, u32[]{:S(2)}) collective-permute-start(bf16[4,2,128,384]{3,2,1,0:T(8,128)(2,1)S(1)} %add_convert_fusion.1), channel_id=1, source_target_pairs={{0,12},{1,131},{16,28},{17,147},{32,44},{33,163},{48,60},{49,179},... | collective-permute-start | bytes 2359304 | tf_op jit(solution)/shard_map/scatter/ppermute | solution.py:29
  70.0 5.5 %collective-permute-done.13 = bf16[4,2,128,384]{3,2,1,0:T(8,128)(2,1)S(1)} collective-permute-done((bf16[4,2,128,384]{3,2,1,0:T(8,128)(2,1)S(1)}, bf16[4,2,128,384]{3,2,1,0:T(8,128)(2,1)S(1)}, u32[]{:S(2)}, u32[]{:S(2)}) %collective-permute-start.13) | collective-permute-done | bytes 786464 | tf_op jit(solution)/shard_map/scatter/ppermute | solution.py:29
  75.5 8.7 %collective-permute-done.15 = bf16[4,2,128,384]{3,2,1,0:T(8,128)(2,1)S(1)} collective-permute-done((bf16[4,2,128,384]{3,2,1,0:T(8,128)(2,1)S(1)}, bf16[4,2,128,384]{3,2,1,0:T(8,128)(2,1)S(1)}, u32[]{:S(2)}, u32[]{:S(2)}) %collective-permute-start.15) | collective-permute-done | bytes 786464 | tf_op jit(solution)/shard_map/scatter/ppermute | solution.py:29
  84.2 2.9 %collective-permute-done.17 = bf16[4,2,128,384]{3,2,1,0:T(8,128)(2,1)S(1)} collective-permute-done((bf16[4,2,128,384]{3,2,1,0:T(8,128)(2,1)S(1)}, bf16[4,2,128,384]{3,2,1,0:T(8,128)(2,1)S(1)}, u32[]{:S(2)}, u32[]{:S(2)}) %collective-permute-start.17) | collective-permute-done | bytes 786464 | tf_op jit(solution)/shard_map/scatter/ppermute | solution.py:29
  87.1 0.5 add_convert_fusion
  87.7 3.2 %collective-permute-start.20 = (bf16[2,128,384]{2,1,0:T(8,128)(2,1)S(1)}, bf16[2,128,384]{2,1,0:T(8,128)(2,1)S(1)}, u32[]{:S(2)}, u32[]{:S(2)}) collective-permute-start(bf16[2,128,384]{2,1,0:T(8,128)(2,1)S(1)} %get-tuple-element.27), channel_id=1, source_target_pairs={{0,130},{1,13},{16,146},{17,29},{32,162},{33,45},{48,178},{49,61},... | collective-permute-start | bytes 589832 | tf_op jit(solution)/shard_map/scatter/ppermute | solution.py:29
  91.0 3.6 %collective-permute-done.18 = bf16[2,128,384]{2,1,0:T(8,128)(2,1)S(1)} collective-permute-done((bf16[2,128,384]{2,1,0:T(8,128)(2,1)S(1)}, bf16[2,128,384]{2,1,0:T(8,128)(2,1)S(1)}, u32[]{:S(2)}, u32[]{:S(2)}) %collective-permute-start.18) | collective-permute-done | bytes 196640 | tf_op jit(solution)/shard_map/scatter/ppermute | solution.py:29
  94.6 1.7 %collective-permute-done.20 = bf16[2,128,384]{2,1,0:T(8,128)(2,1)S(1)} collective-permute-done((bf16[2,128,384]{2,1,0:T(8,128)(2,1)S(1)}, bf16[2,128,384]{2,1,0:T(8,128)(2,1)S(1)}, u32[]{:S(2)}, u32[]{:S(2)}) %collective-permute-start.20) | collective-permute-done | bytes 196640 | tf_op jit(solution)/shard_map/scatter/ppermute | solution.py:29
  96.3 1.9 %collective-permute-done.19 = bf16[2,128,384]{2,1,0:T(8,128)(2,1)S(1)} collective-permute-done((bf16[2,128,384]{2,1,0:T(8,128)(2,1)S(1)}, bf16[2,128,384]{2,1,0:T(8,128)(2,1)S(1)}, u32[]{:S(2)}, u32[]{:S(2)}) %collective-permute-start.19) | collective-permute-done | bytes 196640 | tf_op jit(solution)/shard_map/scatter/ppermute | solution.py:29
  98.4 5.5 %reduce-scatter.2.cloned.1.call-done = bf16[768,256]{1,0:T(8,128)(2,1)} async-done(((bf16[6144,256]{1,0:T(8,128)(2,1)}), bf16[768,256]{1,0:T(8,128)(2,1)}) %reduce-scatter.2.cloned.1.call-update) | async-done | bytes 393232 | tf_op jit(solution)/shard_map/weight_sums/reduce_scatter | solution.py:283
  103.9 1.1 broadcast_select_fusion
  104.9 1.6 %collective-permute-start.22 = (bf16[2,3,4,16,256]{4,3,2,1,0:T(8,128)(2,1)S(1)}, bf16[2,3,4,16,256]{4,3,2,1,0:T(8,128)(2,1)S(1)}, u32[]{:S(2)}, u32[]{:S(2)}) collective-permute-start(bf16[2,3,4,16,256]{4,3,2,1,0:T(8,128)(2,1)S(1)} %bitcast.41), channel_id=1, source_target_pairs={{0,128},{1,129},{16,144},{17,145},{32,160},{33,161},{48,176},{49,1... | collective-permute-start | bytes 589832 | tf_op jit(solution)/shard_map/weight_halves/ppermute | solution.py:29
  106.5 0.7 broadcast_select_fusion.4
  107.2 3.5 %collective-permute-done.22 = bf16[2,3,4,16,256]{4,3,2,1,0:T(8,128)(2,1)S(1)} collective-permute-done((bf16[2,3,4,16,256]{4,3,2,1,0:T(8,128)(2,1)S(1)}, bf16[2,3,4,16,256]{4,3,2,1,0:T(8,128)(2,1)S(1)}, u32[]{:S(2)}, u32[]{:S(2)}) %collective-permute-start.22) | collective-permute-done | bytes 196640 | tf_op jit(solution)/shard_map/weight_halves/ppermute | solution.py:29
  110.7 0.8 fusion.5
  (59 shorter events, 3.0 us)
Async XLA Ops:
  7.2 15.8 %copy-start.3 = (s32[6,4]{0,1:T(4,128)S(1)}, s32[6,4]{0,1:T(4,128)}, u32[]{:S(2)}) copy-start(s32[6,4]{0,1:T(4,128)} %param.11) | copy-start | bytes 292
  7.2 96.7 %reduce-scatter.2.cloned.1.call-start = ((), (), s32[]{:S(2)}) async-start(), calls=%async_computation.1 | async-start | bytes 3538944 | tf_op jit(solution)/shard_map/weight_sums/reduce_scatter | solution.py:283
  8.2 1.4 %collective-permute-start = (bf16[128,384]{1,0:T(8,128)(2,1)S(1)}, bf16[128,384]{1,0:T(8,128)(2,1)S(1)}, u32[]{:S(2)}, u32[]{:S(2)}) collective-permute-start(bf16[128,384]{1,0:T(8,128)(2,1)S(1)} %get-tuple-element.40), channel_id=1, source_target_pairs={{0,1},{1,0},{16,17},{17,16},{32,33},{33,32},{48,49},{49,48},{64,65... | collective-permute-start | bytes 294920 | tf_op jit(solution)/shard_map/gather/ppermute | solution.py:29
  9.6 7.4 %collective-permute-start.2 = (bf16[2,128,384]{2,1,0:T(8,128)(2,1)S(1)}, bf16[2,128,384]{2,1,0:T(8,128)(2,1)S(1)}, u32[]{:S(2)}, u32[]{:S(2)}) collective-permute-start(bf16[2,128,384]{2,1,0:T(8,128)(2,1)S(1)} %get-tuple-element.38), channel_id=1, source_target_pairs={{0,8},{1,3},{16,24},{17,19},{32,40},{33,35},{48,56},{49,51},{64,72... | collective-permute-start | bytes 589832 | tf_op jit(solution)/shard_map/gather/ppermute | solution.py:29
  12.0 7.0 %collective-permute-start.1 = (bf16[2,128,384]{2,1,0:T(8,128)(2,1)S(1)}, bf16[2,128,384]{2,1,0:T(8,128)(2,1)S(1)}, u32[]{:S(2)}, u32[]{:S(2)}) collective-permute-start(bf16[2,128,384]{2,1,0:T(8,128)(2,1)S(1)} %get-tuple-element.38), channel_id=1, source_target_pairs={{0,4},{1,129},{16,20},{17,145},{32,36},{33,161},{48,52},{49,177},{... | collective-permute-start | bytes 589832 | tf_op jit(solution)/shard_map/gather/ppermute | solution.py:29
  12.3 6.7 %collective-permute-start.3 = (bf16[2,128,384]{2,1,0:T(8,128)(2,1)S(1)}, bf16[2,128,384]{2,1,0:T(8,128)(2,1)S(1)}, u32[]{:S(2)}, u32[]{:S(2)}) collective-permute-start(bf16[2,128,384]{2,1,0:T(8,128)(2,1)S(1)} %get-tuple-element.38), channel_id=1, source_target_pairs={{0,12},{1,131},{16,28},{17,147},{32,44},{33,163},{48,60},{49,179},... | collective-permute-start | bytes 589832 | tf_op jit(solution)/shard_map/gather/ppermute | solution.py:29
  19.1 20.2 %collective-permute-start.6 = (bf16[4,2,128,384]{3,2,1,0:T(8,128)(2,1)S(1)}, bf16[4,2,128,384]{3,2,1,0:T(8,128)(2,1)S(1)}, u32[]{:S(2)}, u32[]{:S(2)}) collective-permute-start(bf16[4,2,128,384]{3,2,1,0:T(8,128)(2,1)S(1)} %pad_maximum_fusion.refs_0_), channel_id=1, source_target_pairs={{0,130},{1,13},{16,146},{17,29},{32,162},{33,45},{48,178},{49,61},... | collective-permute-start | bytes 2359304 | tf_op jit(solution)/shard_map/gather/ppermute | solution.py:29
  21.3 18.0 %collective-permute-start.5 = (bf16[4,2,128,384]{3,2,1,0:T(8,128)(2,1)S(1)}, bf16[4,2,128,384]{3,2,1,0:T(8,128)(2,1)S(1)}, u32[]{:S(2)}, u32[]{:S(2)}) collective-permute-start(bf16[4,2,128,384]{3,2,1,0:T(8,128)(2,1)S(1)} %pad_maximum_fusion.refs_0_), channel_id=1, source_target_pairs={{0,2},{1,9},{16,18},{17,25},{32,34},{33,41},{48,50},{49,57},{64,66... | collective-permute-start | bytes 2359304 | tf_op jit(solution)/shard_map/gather/ppermute | solution.py:29
  22.0 21.3 %collective-permute-start.4 = (bf16[4,2,128,384]{3,2,1,0:T(8,128)(2,1)S(1)}, bf16[4,2,128,384]{3,2,1,0:T(8,128)(2,1)S(1)}, u32[]{:S(2)}, u32[]{:S(2)}) collective-permute-start(bf16[4,2,128,384]{3,2,1,0:T(8,128)(2,1)S(1)} %pad_maximum_fusion.refs_0_), channel_id=1, source_target_pairs={{0,128},{1,5},{16,144},{17,21},{32,160},{33,37},{48,176},{49,53},{... | collective-permute-start | bytes 2359304 | tf_op jit(solution)/shard_map/gather/ppermute | solution.py:29
  23.6 22.1 %collective-permute-start.7 = (bf16[4,2,128,384]{3,2,1,0:T(8,128)(2,1)S(1)}, bf16[4,2,128,384]{3,2,1,0:T(8,128)(2,1)}, u32[]{:S(2)}, u32[]{:S(2)}) collective-permute-start(bf16[4,2,128,384]{3,2,1,0:T(8,128)(2,1)S(1)} %pad_maximum_fusion.refs_0_), channel_id=1, source_target_pairs={{0,1},{1,0},{16,17},{17,16},{32,33},{33,32},{48,49},{49,48},{64,65... | collective-permute-start | bytes 2359304 | tf_op jit(solution)/shard_map/gather/ppermute | solution.py:29
  39.3 6.4 %collective-permute-start.10 = (bf16[4,2,128,384]{3,2,1,0:T(8,128)(2,1)S(1)}, bf16[4,2,128,384]{3,2,1,0:T(8,128)(2,1)}, u32[]{:S(2)}, u32[]{:S(2)}) collective-permute-start(bf16[4,2,128,384]{3,2,1,0:T(8,128)(2,1)S(1)} %collective-permute-done.6.refs_3_), channel_id=1, source_target_pairs={{0,1},{1,0},{16,17},{17,16},{32,33},{33,32},{48,49},{49,48},{64,65... | collective-permute-start | bytes 2359304 | tf_op jit(solution)/shard_map/gather/ppermute | solution.py:29
  39.3 6.4 %collective-permute-start.9 = (bf16[4,2,128,384]{3,2,1,0:T(8,128)(2,1)S(1)}, bf16[4,2,128,384]{3,2,1,0:T(8,128)(2,1)}, u32[]{:S(2)}, u32[]{:S(2)}) collective-permute-start(bf16[4,2,128,384]{3,2,1,0:T(8,128)(2,1)S(1)} %collective-permute-done.5.refs_2_), channel_id=1, source_target_pairs={{0,1},{1,0},{16,17},{17,16},{32,33},{33,32},{48,49},{49,48},{64,65... | collective-permute-start | bytes 2359304 | tf_op jit(solution)/shard_map/gather/ppermute | solution.py:29
  43.3 2.5 %collective-permute-start.8 = (bf16[4,2,128,384]{3,2,1,0:T(8,128)(2,1)S(1)}, bf16[4,2,128,384]{3,2,1,0:T(8,128)(2,1)}, u32[]{:S(2)}, u32[]{:S(2)}) collective-permute-start(bf16[4,2,128,384]{3,2,1,0:T(8,128)(2,1)S(1)} %collective-permute-done.4.refs_1_), channel_id=1, source_target_pairs={{0,1},{1,0},{16,17},{17,16},{32,33},{33,32},{48,49},{49,48},{64,65... | collective-permute-start | bytes 2359304 | tf_op jit(solution)/shard_map/gather/ppermute | solution.py:29
  52.7 0.8 copy-start
  53.5 1.0 copy-start.1
  53.5 1.0 copy-start.2
  59.6 3.0 %collective-permute-start.12 = (bf16[4,2,128,384]{3,2,1,0:T(8,128)(2,1)S(1)}, bf16[4,2,128,384]{3,2,1,0:T(8,128)(2,1)S(1)}, u32[]{:S(2)}, u32[]{:S(2)}) collective-permute-start(bf16[4,2,128,384]{3,2,1,0:T(8,128)(2,1)S(1)} %get-tuple-element.20), channel_id=1, source_target_pairs={{0,1},{1,0},{16,17},{17,16},{32,33},{33,32},{48,49},{49,48},{64,65... | collective-permute-start | bytes 2359304 | tf_op jit(solution)/shard_map/scatter/ppermute | solution.py:29
  60.5 5.5 %collective-permute-start.14 = (bf16[4,2,128,384]{3,2,1,0:T(8,128)(2,1)}, bf16[4,2,128,384]{3,2,1,0:T(8,128)(2,1)S(1)}, u32[]{:S(2)}, u32[]{:S(2)}) collective-permute-start(bf16[4,2,128,384]{3,2,1,0:T(8,128)(2,1)} %get-tuple-element.22), channel_id=1, source_target_pairs={{0,1},{1,0},{16,17},{17,16},{32,33},{33,32},{48,49},{49,48},{64,65... | collective-permute-start | bytes 2359304 | tf_op jit(solution)/shard_map/scatter/ppermute | solution.py:29
  60.6 6.4 %collective-permute-start.16 = (bf16[4,2,128,384]{3,2,1,0:T(8,128)(2,1)}, bf16[4,2,128,384]{3,2,1,0:T(8,128)(2,1)S(1)}, u32[]{:S(2)}, u32[]{:S(2)}) collective-permute-start(bf16[4,2,128,384]{3,2,1,0:T(8,128)(2,1)} %get-tuple-element.24), channel_id=1, source_target_pairs={{0,1},{1,0},{16,17},{17,16},{32,33},{33,32},{48,49},{49,48},{64,65... | collective-permute-start | bytes 2359304 | tf_op jit(solution)/shard_map/scatter/ppermute | solution.py:29
  61.1 8.9 %collective-permute-start.11 = (bf16[4,2,128,384]{3,2,1,0:T(8,128)(2,1)S(1)}, bf16[4,2,128,384]{3,2,1,0:T(8,128)(2,1)S(1)}, u32[]{:S(2)}, u32[]{:S(2)}) collective-permute-start(bf16[4,2,128,384]{3,2,1,0:T(8,128)(2,1)S(1)} %get-tuple-element.18), channel_id=1, source_target_pairs={{0,1},{1,0},{16,17},{17,16},{32,33},{33,32},{48,49},{49,48},{64,65... | collective-permute-start | bytes 2359304 | tf_op jit(solution)/shard_map/scatter/ppermute | solution.py:29
  62.8 12.7 %collective-permute-start.13 = (bf16[4,2,128,384]{3,2,1,0:T(8,128)(2,1)S(1)}, bf16[4,2,128,384]{3,2,1,0:T(8,128)(2,1)S(1)}, u32[]{:S(2)}, u32[]{:S(2)}) collective-permute-start(bf16[4,2,128,384]{3,2,1,0:T(8,128)(2,1)S(1)} %add_convert_fusion.3), channel_id=1, source_target_pairs={{0,4},{1,129},{16,20},{17,145},{32,36},{33,161},{48,52},{49,177},{... | collective-permute-start | bytes 2359304 | tf_op jit(solution)/shard_map/scatter/ppermute | solution.py:29
  66.2 18.0 %collective-permute-start.15 = (bf16[4,2,128,384]{3,2,1,0:T(8,128)(2,1)S(1)}, bf16[4,2,128,384]{3,2,1,0:T(8,128)(2,1)S(1)}, u32[]{:S(2)}, u32[]{:S(2)}) collective-permute-start(bf16[4,2,128,384]{3,2,1,0:T(8,128)(2,1)S(1)} %add_convert_fusion.2), channel_id=1, source_target_pairs={{0,8},{1,3},{16,24},{17,19},{32,40},{33,35},{48,56},{49,51},{64,72... | collective-permute-start | bytes 2359304 | tf_op jit(solution)/shard_map/scatter/ppermute | solution.py:29
  67.3 19.8 %collective-permute-start.17 = (bf16[4,2,128,384]{3,2,1,0:T(8,128)(2,1)S(1)}, bf16[4,2,128,384]{3,2,1,0:T(8,128)(2,1)S(1)}, u32[]{:S(2)}, u32[]{:S(2)}) collective-permute-start(bf16[4,2,128,384]{3,2,1,0:T(8,128)(2,1)S(1)} %add_convert_fusion.1), channel_id=1, source_target_pairs={{0,12},{1,131},{16,28},{17,147},{32,44},{33,163},{48,60},{49,179},... | collective-permute-start | bytes 2359304 | tf_op jit(solution)/shard_map/scatter/ppermute | solution.py:29
  87.6 7.0 %collective-permute-start.18 = (bf16[2,128,384]{2,1,0:T(8,128)(2,1)S(1)}, bf16[2,128,384]{2,1,0:T(8,128)(2,1)S(1)}, u32[]{:S(2)}, u32[]{:S(2)}) collective-permute-start(bf16[2,128,384]{2,1,0:T(8,128)(2,1)S(1)} %get-tuple-element.26), channel_id=1, source_target_pairs={{0,128},{1,5},{16,144},{17,21},{32,160},{33,37},{48,176},{49,53},{... | collective-permute-start | bytes 589832 | tf_op jit(solution)/shard_map/scatter/ppermute | solution.py:29
  87.7 8.5 %collective-permute-start.20 = (bf16[2,128,384]{2,1,0:T(8,128)(2,1)S(1)}, bf16[2,128,384]{2,1,0:T(8,128)(2,1)S(1)}, u32[]{:S(2)}, u32[]{:S(2)}) collective-permute-start(bf16[2,128,384]{2,1,0:T(8,128)(2,1)S(1)} %get-tuple-element.27), channel_id=1, source_target_pairs={{0,130},{1,13},{16,146},{17,29},{32,162},{33,45},{48,178},{49,61},... | collective-permute-start | bytes 589832 | tf_op jit(solution)/shard_map/scatter/ppermute | solution.py:29
  91.0 7.2 %collective-permute-start.19 = (bf16[2,128,384]{2,1,0:T(8,128)(2,1)S(1)}, bf16[2,128,384]{2,1,0:T(8,128)(2,1)S(1)}, u32[]{:S(2)}, u32[]{:S(2)}) collective-permute-start(bf16[2,128,384]{2,1,0:T(8,128)(2,1)S(1)} %get-tuple-element.28), channel_id=1, source_target_pairs={{0,2},{1,9},{16,18},{17,25},{32,34},{33,41},{48,50},{49,57},{64,66... | collective-permute-start | bytes 589832 | tf_op jit(solution)/shard_map/scatter/ppermute | solution.py:29
  98.3 8.2 %collective-permute-start.21 = (bf16[128,384]{1,0:T(8,128)(2,1)S(1)}, bf16[128,384]{1,0:T(8,128)(2,1)S(1)}, u32[]{:S(2)}, u32[]{:S(2)}) collective-permute-start(bf16[128,384]{1,0:T(8,128)(2,1)S(1)} %slice_bitcast_fusion.4), channel_id=1, source_target_pairs={{0,1},{1,0},{16,17},{17,16},{32,33},{33,32},{48,49},{49,48},{64,65... | collective-permute-start | bytes 294920 | tf_op jit(solution)/shard_map/scatter/ppermute | solution.py:29
  104.9 5.8 %collective-permute-start.22 = (bf16[2,3,4,16,256]{4,3,2,1,0:T(8,128)(2,1)S(1)}, bf16[2,3,4,16,256]{4,3,2,1,0:T(8,128)(2,1)S(1)}, u32[]{:S(2)}, u32[]{:S(2)}) collective-permute-start(bf16[2,3,4,16,256]{4,3,2,1,0:T(8,128)(2,1)S(1)} %bitcast.41), channel_id=1, source_target_pairs={{0,128},{1,129},{16,144},{17,145},{32,160},{33,161},{48,176},{49,1... | collective-permute-start | bytes 589832 | tf_op jit(solution)/shard_map/weight_halves/ppermute | solution.py:29
Sparse Core Ops, SparseCore 0:
  53.7 50.1 reduce-scatter.1

commit v2 on v0

v2 whole, which is shorter than its diff:
```python
import jax
import jax.numpy as jnp
from jax import lax
from jax.experimental import pallas as pl
from jax.experimental.pallas import tpu as pltpu
from jax.sharding import Mesh, PartitionSpec as P

BLK = 256
HALF = 128
WIDE = 384
K = 4
NH = 6
NB = NH * K
AXES = ("ylo", "z", "x", "yhi", "core")
VMEM_LIMIT = 40 * 1024 * 1024
BF16, F32 = jnp.bfloat16, jnp.float32


def device_id(x, y, z, c):
    return ((y % 2) * 8 + z) * 16 + x * 4 + (y // 2) * 2 + c


def permute(value, target):
    pairs = []
    for x in range(4):
        for y in range(4):
            for z in range(8):
                for c in range(2):
                    tx, ty, tz, tc = target(x, y, z, c)
                    pairs.append((device_id(x, y, z, c), device_id(tx % 4, ty % 4, tz % 8, tc)))
    return lax.ppermute(value, AXES, pairs)


def other_core(x, y, z, c):
    return x, y, z, 1 - c


def ahead_z(x, y, z, c):
    return x, y, (z + 1 if c == 0 else z - 1), c


def back_z(x, y, z, c):
    return x, y, (z - 1 if c == 0 else z + 1), c


def gather_first(step):
    return lambda x, y, z, c: (x + step, y, z, c) if c == 0 else (x, y + step, z, c)


def gather_second(step):
    return lambda x, y, z, c: (x, y + step, z, c) if c == 0 else (x + step, y, z, c)


def along_x(step):
    return lambda x, y, z, c: (x + step, y, z, c)


def across_y(x, y, z, c):
    return x, y + 2, z, c


def place():
    return [lax.axis_index(a) for a in AXES]


def unit_owner(unit):
    return (unit * 43) >> 7


def gathered_quarter(all_ref, kind, unit, token_half, x, y, core):
    t = unit_owner(unit)
    lane = (unit - 3 * t) * HALF
    c = t & 1
    dx = (x - (t >> 2)) & 3
    dy = (y - ((t & 2) + token_half)) & 3
    first = jnp.where(c == 0, dx, dy)
    second = jnp.where(c == 0, dy, dx)
    return all_ref[kind, c ^ core, second, first, :, pl.ds(pl.multiple_of(lane, HALF), HALF)]


def gathered_block(all_ref, kind, b, x, y, core):
    rows = []
    for h in range(2):
        cols = [gathered_quarter(all_ref, kind, 2 * b + u, h, x, y, core) for u in range(2)]
        rows.append(jnp.concatenate(cols, axis=1))
    return jnp.concatenate(rows, axis=0)


def dot(a, b, a_dim, b_dim):
    return lax.dot_general(a, b, (((a_dim,), (b_dim,)), ((), ())), preferred_element_type=F32)


def grads_kernel(up_idx, down_idx, *refs):
    parts, (up_hbm, down_hbm) = refs[0:8], refs[8:10]
    hid_ref, pg_ref, dw_ref, far_ref = refs[10:14]
    all_ref, up_ref, down_ref, pre_ref, sem = refs[14:]
    ylo, z, x, yhi, core = place()
    y = yhi * 2 + ylo

    def fetch(kind):
        for slot in range(2):
            for i, e in enumerate((0, 1, 3, 2)):
                pltpu.make_async_copy(
                    parts[4 * slot + i].at[:, kind], all_ref.at[kind, slot, e], sem.at[kind]
                ).start()

    def await_all(ref, i):
        pltpu.make_async_copy(ref, ref, sem.at[i]).wait()

    fetch(0)
    up_copy = pltpu.make_async_copy(up_hbm, up_ref, sem.at[2])
    up_copy.start()
    fetch(1)
    down_copy = pltpu.make_async_copy(down_hbm, down_ref, sem.at[3])
    down_copy.start()

    def store_rows(g, j, value):
        value = value.astype(BF16)
        for i in range(8):
            r = jnp.where(core == 0, i - z, z - i) & 7
            dw_ref[r, g, j] = value[i * 16 : i * 16 + 16]

    await_all(all_ref.at[0], 0)
    up_copy.wait()
    for n in range(NH):
        acc = jnp.zeros((BLK, BLK), F32)
        for k in range(K):
            tok = gathered_block(all_ref, 0, up_idx[n * K + k], x, y, core)
            acc += dot(tok, up_ref[n, k], 1, 0)
        pre_ref[n] = acc
        hid_ref[n] = (acc * jax.nn.sigmoid(acc)).astype(BF16)
    await_all(all_ref.at[1], 1)
    down_copy.wait()
    lanes = pl.ds(pl.multiple_of(ylo * HALF, HALF), HALF)
    for n in range(NH):
        hidden = hid_ref[n, :, lanes]
        acc = jnp.zeros((BLK, BLK), F32)
        for k in range(K):
            cot = gathered_block(all_ref, 1, down_idx[n * K + k], x, y, core)
            acc += dot(cot, down_ref[n, k], 1, 1)
            store_rows(1, n * K + k, dot(hidden, cot, 0, 0))
        pre = pre_ref[n]
        sig = jax.nn.sigmoid(pre)
        pre_grad = (acc * (sig * (1.0 + pre * (1.0 - sig)))).astype(BF16)
        pg_ref[n] = pre_grad
        for k in range(K):
            unit = 2 * up_idx[n * K + k] + ylo
            tok = jnp.concatenate(
                [gathered_quarter(all_ref, 0, unit, h, x, y, core) for h in range(2)], axis=0
            )
            store_rows(0, n * K + k, dot(tok, pre_grad, 0, 0))
    far_ref[...] = dw_ref[4]


def terms_kernel(up_idx, down_idx, hid_ref, pg_ref, up_ref, down_ref, *refs):
    keep, give, acc = refs[0:4], refs[4:6], refs[6]
    ylo, z, x, yhi, core = place()
    acc[...] = jnp.zeros_like(acc)

    def add(kind, b, value):
        for u in range(2):
            unit = 2 * b + u
            t = unit_owner(unit)
            lane = (unit - 3 * t) * HALF
            dx = ((t >> 2) - x) & 3
            dy = ((t >> 1) & 1) ^ yhi
            where = ((((t & 1) ^ core) * 4 + dx) * 2 + dy) * 2 + kind
            acc[where, :, pl.ds(pl.multiple_of(lane, HALF), HALF)] += value[
                :, u * HALF : (u + 1) * HALF
            ]

    rows = pl.ds(pl.multiple_of(ylo * HALF, HALF), HALF)
    for n in range(NH):
        hidden = hid_ref[n, rows]
        pre_grad = pg_ref[n, rows]
        for k in range(K):
            add(0, down_idx[n * K + k], dot(hidden, down_ref[n, k], 1, 0))
            add(1, up_idx[n * K + k], dot(pre_grad, up_ref[n, k], 1, 1))
    for dx in range(4):
        for dy in range(2):
            for kind in range(2):
                keep[dx][dy, kind] = acc[(dx * 2 + dy) * 2 + kind].astype(BF16)
                other = acc[((4 + dx) * 2 + dy) * 2 + kind].astype(BF16)
                give[0 if dx in (1, 2) else 1][dx // 2, dy, kind] = other


def specs(space, count):
    return [pl.BlockSpec(memory_space=space)] * count


def run(kernel, name, args, in_specs, out_shape, scratch, flops, moved):
    return pl.pallas_call(
        kernel,
        out_shape=tuple(out_shape),
        in_specs=in_specs,
        out_specs=tuple(specs(pltpu.VMEM, len(out_shape))),
        scratch_shapes=scratch,
        compiler_params=pltpu.CompilerParams(vmem_limit_bytes=VMEM_LIMIT),
        cost_estimate=pl.CostEstimate(flops=flops, bytes_accessed=moved, transcendentals=0),
        name=name,
    )(*args)


def shape(*dims, dtype=BF16):
    return jax.ShapeDtypeStruct(dims, dtype)


def wide_sum(*terms):
    total = terms[0].astype(F32)
    for term in terms[1:]:
        total = total + term.astype(F32)
    return total.astype(BF16)


def on_device(tokens, cotangent, up_blocks, up_index, down_blocks, down_index):
    up_idx, down_idx = up_index.reshape(-1), down_index.reshape(-1)

    with jax.named_scope("gather"):
        own = jnp.stack([tokens, cotangent])
        line = jnp.stack([own] + [permute(own, gather_first(d)) for d in (1, 2, 3)])
        mine = [line] + [permute(line, gather_second(e)) for e in (1, 3, 2)]
        theirs = [permute(part, other_core) for part in mine]

    piece = HALF * WIDE * 2
    matmul = 2 * BLK**3
    smem, vmem, anyw = pltpu.SMEM, pltpu.VMEM, pl.ANY
    hidden, pre_grad, parts, far = run(
        grads_kernel,
        "grads",
        (up_idx, down_idx, *mine, *theirs, up_blocks, down_blocks),
        specs(smem, 2) + specs(anyw, 10),
        [
            shape(NH, BLK, BLK),
            shape(NH, BLK, BLK),
            shape(8, 2, NB, 16, BLK),
            shape(2, NB, 16, BLK),
        ],
        [
            pltpu.VMEM((2, 2, 4, 4, HALF, WIDE), BF16),
            pltpu.VMEM((NH, K, BLK, BLK), BF16),
            pltpu.VMEM((NH, K, BLK, BLK), BF16),
            pltpu.VMEM((NH, BLK, BLK), F32),
            pltpu.SemaphoreType.DMA((4,)),
        ],
        72 * matmul,
        128 * piece,
    )
    with jax.named_scope("weight_sums"):
        ahead = permute(far, ahead_z)

    *keep, give_a, give_b = run(
        terms_kernel,
        "terms",
        (up_idx, down_idx, hidden, pre_grad, up_blocks, down_blocks),
        specs(smem, 2) + specs(vmem, 4),
        [shape(2, 2, HALF, WIDE)] * 4 + [shape(2, 2, 2, HALF, WIDE)] * 2,
        [pltpu.VMEM((32, HALF, WIDE), F32)],
        24 * matmul,
        96 * piece,
    )
    tie = lax.optimization_barrier
    with jax.named_scope("scatter"):
        got_a, got_b = permute(give_a, other_core), permute(give_b, other_core)
        sums = [wide_sum(keep[dx], got) for dx, got in ((1, got_a[0]), (2, got_a[1]), (3, got_b[1]))]
        ahead = wide_sum(parts[3], ahead)
        *sums, ahead, back = tie((*sums, ahead, parts[5]))
    with jax.named_scope("weight_sums"):
        ahead, back = permute(ahead, ahead_z), permute(back, back_z)
    with jax.named_scope("scatter"):
        sent = [permute(total, along_x(dx)) for dx, total in zip((1, 2, 3), sums)]
    with jax.named_scope("weight_sums"):
        ahead, back = tie((wide_sum(parts[2], ahead), wide_sum(parts[6], back)))
        *sent, _, _ = tie((*sent, ahead, back))
        ahead, back = permute(ahead, ahead_z), permute(back, back_z)
    with jax.named_scope("scatter"):
        line_sum = wide_sum(keep[0], got_b[0], *sent)
        across = permute(line_sum[1], across_y)
    with jax.named_scope("weight_sums"):
        ahead, back = tie((wide_sum(parts[1], ahead), wide_sum(parts[7], back)))
        across, _, _ = tie((across, ahead, back))
        ahead, back = permute(ahead, ahead_z), permute(back, back_z)
        weight_grads = wide_sum(parts[0], ahead, back)
    with jax.named_scope("scatter"):
        final = wide_sum(line_sum[0], across)

    rows = (NH, K, 16, BLK)
    return final[0], final[1], weight_grads[0].reshape(rows), weight_grads[1].reshape(rows)


def solution(mesh):
    fine = Mesh(mesh.devices.reshape(2, 8, 4, 2, 2), AXES)
    dp, tensor = ("ylo", "z"), ("x", "yhi", "core")
    in_specs = (
        P(dp, tensor),
        P(dp, tensor),
        P(tensor, None, None, None),
        P(tensor, None),
        P(tensor, None, None, None),
        P(tensor, None),
    )
    out_specs = (
        P(dp, tensor),
        P(dp, tensor),
        P(tensor, None, dp, None),
        P(tensor, None, dp, None),
    )
    return jax.shard_map(
        on_device, mesh=fine, in_specs=in_specs, out_specs=out_specs, check_vma=False
    )
```

time: 537 us -> 104 us (0.19); the launches traced: 528 us -> 104 us
  waiting for transfers between devices: 446 us -> 44.7 us
  starting transfers between devices: 0.43 us -> 40.7 us
  local copies, waits for them, and re-layouts: 37.3 us -> 5.1 us
  matrix products: 26.2 us -> 0 us
  between operations: 14.9 us -> 0.78 us
  Pallas kernels: 0 us -> 10 us
    unnamed x9 -> x0, waiting for transfers between devices: 264 us -> none
    all_gather x2 -> x0, waiting for transfers between devices: 106 us -> none  [the longest x1 54.8 us: on_device(): token_panel = lax.all_gather(tokens, 'tensor', axis=1, tiled=True)]
    reduce_scatter x1 -> x0, waiting for transfers between devices: 76 us -> none  [on_device(): lax.psum_scatter(up_local.astype(jnp.bfloat16), 'dp', scatter_dimension=2...]
    ppermute x0 -> x23, waiting for transfers between devices: none -> 44.7 us  [permute(): return lax.ppermute(value, AXES, pairs)]
    ppermute x0 -> x23, starting transfers between devices: none -> 40.7 us  [permute(): return lax.ppermute(value, AXES, pairs)]
    dot_general x8 -> x0, matrix products: 26.2 us -> none  [the longest x2 9.09 us: place_blocks(): jnp.einsum('tjd,jb->tbd', partial_terms.reshape(row_count, local_blocks *...]
    unnamed x21 -> x8, local copies, waits for them, and re-layouts: 19.2 us -> 3.43 us
    pallas_call x0 -> x2, Pallas kernels: none -> 10 us  [run(): pl.pallas_call(kernel, out_shape=tuple(out_shape), in_specs=in_specs, out...]
  transfers between devices with their start and end apart: 6 -> 23, of which waited for: 6 -> 14; matrix products, arithmetic and copies ran while one was open for 7% -> 3% of each run, Pallas kernels for 0% -> 0%
where the time goes in v2:
time: 104 us
  waiting for transfers between devices  44.7 us (43%)
  starting transfers between devices  40.7 us (39%)
  Pallas kernels  10 us (10%)
  local copies, waits for them, and re-layouts  5.1 us (5%)
  other arithmetic  2.4 us (2%)
    ppermute x23, waiting for transfers between devices, permute(): return lax.ppermute(value, AXES, pairs)  44.7 us
    ppermute x23, starting transfers between devices, permute(): return lax.ppermute(value, AXES, pairs)  40.7 us
    pallas_call x2, Pallas kernels, run(): pl.pallas_call(kernel, out_shape=tuple(out_shape), in_specs=in_specs, out...  10 us
    unnamed x8, local copies, waits for them, and re-layouts  3.43 us
  transfers between devices with their start and end apart: 23, of which 14 were waited for; matrix products, arithmetic and copies ran while one was open for 3% of the time, Pallas kernels for 0%

profile of v2, /device:TPU:1, one launch (start us, length us, event | category | flops | bytes accessed | tf_op | source)
XLA Modules:
  0.0 103.8 jit_solution(13957085682375403389)
XLA Ops:
  0.6 1.0 fusion.15
  1.6 3.8 %collective-permute-start.1 = (bf16[2,128,384]{2,1,0:T(8,128)(2,1)S(1)}, bf16[2,128,384]{2,1,0:T(8,128)(2,1)S(1)}, u32[]{:S(2)}, u32[]{:S(2)}) collective-permute-start(bf16[2,128,384]{2,1,0:T(8,128)(2,1)S(1)} %get-tuple-element.61), channel_id=1, source_target_pairs={{0,8},{1,3},{16,24},{17,19},{32,40},{33,35},{48,56},{49,51},{64,72... | collective-permute-start | bytes 589832 | tf_op jit(solution)/shard_map/gather/ppermute | solution.py:31
  5.4 0.4 collective-permute-start
  5.8 2.3 %collective-permute-start.2 = (bf16[2,128,384]{2,1,0:T(8,128)(2,1)S(1)}, bf16[2,128,384]{2,1,0:T(8,128)(2,1)S(1)}, u32[]{:S(2)}, u32[]{:S(2)}) collective-permute-start(bf16[2,128,384]{2,1,0:T(8,128)(2,1)S(1)} %get-tuple-element.61), channel_id=1, source_target_pairs={{0,12},{1,131},{16,28},{17,147},{32,44},{33,163},{48,60},{49,179},... | collective-permute-start | bytes 589832 | tf_op jit(solution)/shard_map/gather/ppermute | solution.py:31
  8.1 0.4 collective-permute-done.1
  8.5 3.0 %collective-permute-done = bf16[2,128,384]{2,1,0:T(8,128)(2,1)S(1)} collective-permute-done((bf16[2,128,384]{2,1,0:T(8,128)(2,1)S(1)}, bf16[2,128,384]{2,1,0:T(8,128)(2,1)S(1)}, u32[]{:S(2)}, u32[]{:S(2)}) %collective-permute-start) | collective-permute-done | bytes 196640 | tf_op jit(solution)/shard_map/gather/ppermute | solution.py:31
  11.5 0.1 pad_maximum_fusion.refs_0_
  11.6 2.7 %collective-permute-start.5 = (bf16[4,2,128,384]{3,2,1,0:T(8,128)(2,1)S(1)}, bf16[4,2,128,384]{3,2,1,0:T(8,128)(2,1)S(1)}, u32[]{:S(2)}, u32[]{:S(2)}) collective-permute-start(bf16[4,2,128,384]{3,2,1,0:T(8,128)(2,1)S(1)} %pad_maximum_fusion.refs_0_), channel_id=1, source_target_pairs={{0,2},{1,9},{16,18},{17,25},{32,34},{33,41},{48,50},{49,57},{64,66... | collective-permute-start | bytes 2359304 | tf_op jit(solution)/shard_map/gather/ppermute | solution.py:31
  14.3 0.9 collective-permute-start.4
  15.1 0.6 collective-permute-start.3
  15.7 2.8 %collective-permute-start.6 = (bf16[4,2,128,384]{3,2,1,0:T(8,128)(2,1)S(1)}, bf16[4,2,128,384]{3,2,1,0:T(8,128)(2,1)}, u32[]{:S(2)}, u32[]{:S(2)}) collective-permute-start(bf16[4,2,128,384]{3,2,1,0:T(8,128)(2,1)S(1)} %pad_maximum_fusion.refs_0_), channel_id=1, source_target_pairs={{0,1},{1,0},{16,17},{17,16},{32,33},{33,32},{48,49},{49,48},{64,65... | collective-permute-start | bytes 2359304 | tf_op jit(solution)/shard_map/gather/ppermute | solution.py:31
  18.5 5.8 %collective-permute-done.5.refs_3_ = bf16[4,2,128,384]{3,2,1,0:T(8,128)(2,1)S(1)} collective-permute-done((bf16[4,2,128,384]{3,2,1,0:T(8,128)(2,1)S(1)}, bf16[4,2,128,384]{3,2,1,0:T(8,128)(2,1)S(1)}, u32[]{:S(2)}, u32[]{:S(2)}) %collective-permute-start.5) | collective-permute-done | bytes 786464 | tf_op jit(solution)/shard_map/gather/ppermute | solution.py:31
  24.4 3.7 %collective-permute-start.9 = (bf16[4,2,128,384]{3,2,1,0:T(8,128)(2,1)S(1)}, bf16[4,2,128,384]{3,2,1,0:T(8,128)(2,1)}, u32[]{:S(2)}, u32[]{:S(2)}) collective-permute-start(bf16[4,2,128,384]{3,2,1,0:T(8,128)(2,1)S(1)} %collective-permute-done.5.refs_3_), channel_id=1, source_target_pairs={{0,1},{1,0},{16,17},{17,16},{32,33},{33,32},{48,49},{49,48},{64,65... | collective-permute-start | bytes 2359304 | tf_op jit(solution)/shard_map/gather/ppermute | solution.py:31
  28.0 4.8 %collective-permute-done.4.refs_2_ = bf16[4,2,128,384]{3,2,1,0:T(8,128)(2,1)S(1)} collective-permute-done((bf16[4,2,128,384]{3,2,1,0:T(8,128)(2,1)S(1)}, bf16[4,2,128,384]{3,2,1,0:T(8,128)(2,1)S(1)}, u32[]{:S(2)}, u32[]{:S(2)}) %collective-permute-start.4) | collective-permute-done | bytes 786464 | tf_op jit(solution)/shard_map/gather/ppermute | solution.py:31
  32.9 2.8 %collective-permute-start.8 = (bf16[4,2,128,384]{3,2,1,0:T(8,128)(2,1)S(1)}, bf16[4,2,128,384]{3,2,1,0:T(8,128)(2,1)}, u32[]{:S(2)}, u32[]{:S(2)}) collective-permute-start(bf16[4,2,128,384]{3,2,1,0:T(8,128)(2,1)S(1)} %collective-permute-done.4.refs_2_), channel_id=1, source_target_pairs={{0,1},{1,0},{16,17},{17,16},{32,33},{33,32},{48,49},{49,48},{64,65... | collective-permute-start | bytes 2359304 | tf_op jit(solution)/shard_map/gather/ppermute | solution.py:31
  35.6 0.7 collective-permute-start.7
  36.4 0.8 copy.12
  37.2 0.8 copy.13
  38.1 0.7 collective-permute-done.7.refs_5_
  38.8 1.9 %copy-done = bf16[6,4,256,256]{3,2,1,0:T(8,128)(2,1)S(1)} copy-done((bf16[6,4,256,256]{3,2,1,0:T(8,128)(2,1)S(1)}, bf16[6,4,256,256]{3,2,1,0:T(8,128)(2,1)}, u32[]{:S(2)}) %copy-start) | copy-done | bytes 3145752
  40.7 6.9 %grads.1 = (bf16[6,256,256]{2,1,0:T(8,128)(2,1)S(1)}, bf16[6,256,256]{2,1,0:T(8,128)(2,1)S(1)}, bf16[8,2,24,16,256]{4,3,2,1,0:T(8,128)(2,1)S(1)}, bf16[2,24,16,256]{3,2,1,0:T(8,128)(2,1)S(1)}) custom-call(s32[24]{0:T(128)S(1)} %reshape.36.up_idx, s32[24]{0:T(128)S(1)} %reshape.37.down_idx, bf16[4,2,128,384]{3,2,1,0:T(8,128)(2,1)S(1)} %pad_maximum_fusion.refs_0_, ...), custom_call_target="tpu_custom_call" | custom-call | flops 2415919104 | bytes 12582912 | tf_op jit(solution)/shard_map/grads/pallas_call | solution.py:192
  47.6 3.1 %terms.1 = (bf16[2,2,128,384]{3,2,1,0:T(8,128)(2,1)S(1)}, bf16[2,2,128,384]{3,2,1,0:T(8,128)(2,1)S(1)}, bf16[2,2,128,384]{3,2,1,0:T(8,128)(2,1)S(1)}, bf16[2,2,1...) custom-call(s32[24]{0:T(128)S(1)} %reshape.36.up_idx, ...), custom_call_target="tpu_custom_call" | custom-call | flops 805306368 | bytes 9437184 | tf_op jit(solution)/shard_map/terms/pallas_call | solution.py:192
  50.8 0.5 collective-permute-start.10
  51.2 5.6 %collective-permute-start.12 = (bf16[2,24,16,256]{3,2,1,0:T(8,128)(2,1)S(1)}, bf16[2,24,16,256]{3,2,1,0:T(8,128)(2,1)S(1)}, u32[]{:S(2)}, u32[]{:S(2)}) collective-permute-start(bf16[2,24,16,256]{3,2,1,0:T(8,128)(2,1)S(1)} %get-tuple-element.36), channel_id=1, source_target_pairs={{0,16},{1,113},{16,32},{17,1},{32,48},{33,17},{48,64},{49,33},{64,... | collective-permute-start | bytes 1179656 | tf_op jit(solution)/shard_map/weight_sums/ppermute | solution.py:31
  56.8 4.7 %collective-permute-done.12 = bf16[2,24,16,256]{3,2,1,0:T(8,128)(2,1)S(1)} collective-permute-done((bf16[2,24,16,256]{3,2,1,0:T(8,128)(2,1)S(1)}, bf16[2,24,16,256]{3,2,1,0:T(8,128)(2,1)S(1)}, u32[]{:S(2)}, u32[]{:S(2)}) %collective-permute-start.12) | collective-permute-done | bytes 393248 | tf_op jit(solution)/shard_map/weight_sums/ppermute | solution.py:31
  61.5 0.1 fusion.6
  61.6 0.1 fusion.7
  61.8 0.2 fusion.8
  62.0 3.2 %collective-permute-start.16 = (bf16[2,24,16,256]{3,2,1,0:T(8,128)(2,1)S(1)}, bf16[2,24,16,256]{3,2,1,0:T(8,128)(2,1)S(1)}, u32[]{:S(2)}, u32[]{:S(2)}) collective-permute-start(bf16[2,24,16,256]{3,2,1,0:T(8,128)(2,1)S(1)} %fusion.6), channel_id=1, source_target_pairs={{0,16},{1,113},{16,32},{17,1},{32,48},{33,17},{48,64},{49,33},{64,... | collective-permute-start | bytes 1179656 | tf_op jit(solution)/shard_map/weight_sums/ppermute | solution.py:31
  65.2 0.7 collective-permute-start.13
  65.8 3.5 %collective-permute-start.14 = (bf16[2,2,128,384]{3,2,1,0:T(8,128)(2,1)S(1)}, bf16[2,2,128,384]{3,2,1,0:T(8,128)(2,1)S(1)}, u32[]{:S(2)}, u32[]{:S(2)}) collective-permute-start(bf16[2,2,128,384]{3,2,1,0:T(8,128)(2,1)S(1)} %get-tuple-element.38), channel_id=1, source_target_pairs={{0,8},{1,9},{16,24},{17,25},{32,40},{33,41},{48,56},{49,57},{64,72... | collective-permute-start | bytes 1179656 | tf_op jit(solution)/shard_map/scatter/ppermute | solution.py:31
  69.3 3.0 %collective-permute-done.16 = bf16[2,24,16,256]{3,2,1,0:T(8,128)(2,1)S(1)} collective-permute-done((bf16[2,24,16,256]{3,2,1,0:T(8,128)(2,1)S(1)}, bf16[2,24,16,256]{3,2,1,0:T(8,128)(2,1)S(1)}, u32[]{:S(2)}, u32[]{:S(2)}) %collective-permute-start.16) | collective-permute-done | bytes 393248 | tf_op jit(solution)/shard_map/weight_sums/ppermute | solution.py:31
  72.3 4.0 %collective-permute-done.17 = bf16[2,24,16,256]{3,2,1,0:T(8,128)(2,1)S(1)} collective-permute-done((bf16[2,24,16,256]{3,2,1,0:T(8,128)(2,1)S(1)}, bf16[2,24,16,256]{3,2,1,0:T(8,128)(2,1)S(1)}, u32[]{:S(2)}, u32[]{:S(2)}) %collective-permute-start.17) | collective-permute-done | bytes 393248 | tf_op jit(solution)/shard_map/weight_sums/ppermute | solution.py:31
  76.3 0.2 fusion.4
  76.5 0.3 collective-permute-start.19
  76.8 1.5 %collective-permute-start.20 = (bf16[2,24,16,256]{3,2,1,0:T(8,128)(2,1)S(1)}, bf16[2,24,16,256]{3,2,1,0:T(8,128)(2,1)S(1)}, u32[]{:S(2)}, u32[]{:S(2)}) collective-permute-start(bf16[2,24,16,256]{3,2,1,0:T(8,128)(2,1)S(1)} %get-tuple-element.43), channel_id=1, source_target_pairs={{0,112},{1,17},{16,0},{17,33},{32,16},{33,49},{48,32},{49,65},{64,... | collective-permute-start | bytes 1179656 | tf_op jit(solution)/shard_map/weight_sums/ppermute | solution.py:31
  78.3 7.0 %collective-permute-done.14 = bf16[2,2,128,384]{3,2,1,0:T(8,128)(2,1)S(1)} collective-permute-done((bf16[2,2,128,384]{3,2,1,0:T(8,128)(2,1)S(1)}, bf16[2,2,128,384]{3,2,1,0:T(8,128)(2,1)S(1)}, u32[]{:S(2)}, u32[]{:S(2)}) %collective-permute-start.14) | collective-permute-done | bytes 393248 | tf_op jit(solution)/shard_map/scatter/ppermute | solution.py:31
  85.3 0.4 collective-permute-done.15
  85.7 0.3 fusion.13
  86.0 1.6 %collective-permute-start.18 = (bf16[2,128,384]{2,1,0:T(8,128)(2,1)S(1)}, bf16[2,128,384]{2,1,0:T(8,128)(2,1)S(1)}, u32[]{:S(2)}, u32[]{:S(2)}) collective-permute-start(bf16[2,128,384]{2,1,0:T(8,128)(2,1)S(1)} %slice_bitcast_fusion.5), channel_id=1, source_target_pairs={{0,2},{1,3},{16,18},{17,19},{32,34},{33,35},{48,50},{49,51},{64,66... | collective-permute-start | bytes 589832 | tf_op jit(solution)/shard_map/scatter/ppermute | solution.py:31
  87.7 0.8 collective-permute-done.20
  88.5 0.2 fusion.2
  88.7 3.4 %collective-permute-start.21 = (bf16[2,24,16,256]{3,2,1,0:T(8,128)(2,1)S(1)}, bf16[2,24,16,256]{3,2,1,0:T(8,128)(2,1)S(1)}, u32[]{:S(2)}, u32[]{:S(2)}) collective-permute-start(bf16[2,24,16,256]{3,2,1,0:T(8,128)(2,1)S(1)} %get-tuple-element.47), channel_id=1, source_target_pairs={{0,16},{1,113},{16,32},{17,1},{32,48},{33,17},{48,64},{49,33},{64,... | collective-permute-start | bytes 1179656 | tf_op jit(solution)/shard_map/weight_sums/ppermute | solution.py:31
  92.1 0.7 slice_bitcast_fusion.7
  92.8 6.5 %collective-permute-done.21 = bf16[2,24,16,256]{3,2,1,0:T(8,128)(2,1)S(1)} collective-permute-done((bf16[2,24,16,256]{3,2,1,0:T(8,128)(2,1)S(1)}, bf16[2,24,16,256]{3,2,1,0:T(8,128)(2,1)S(1)}, u32[]{:S(2)}, u32[]{:S(2)}) %collective-permute-start.21) | collective-permute-done | bytes 393248 | tf_op jit(solution)/shard_map/weight_sums/ppermute | solution.py:31
  99.3 3.5 %collective-permute-done.22 = bf16[2,24,16,256]{3,2,1,0:T(8,128)(2,1)S(1)} collective-permute-done((bf16[2,24,16,256]{3,2,1,0:T(8,128)(2,1)S(1)}, bf16[2,24,16,256]{3,2,1,0:T(8,128)(2,1)S(1)}, u32[]{:S(2)}, u32[]{:S(2)}) %collective-permute-start.22) | collective-permute-done | bytes 393248 | tf_op jit(solution)/shard_map/weight_sums/ppermute | solution.py:31
  102.8 0.2 fusion.1
  103.0 0.8 fusion.16
  (24 shorter events, 0.4 us)
Async XLA Ops:
  1.6 6.9 %collective-permute-start.1 = (bf16[2,128,384]{2,1,0:T(8,128)(2,1)S(1)}, bf16[2,128,384]{2,1,0:T(8,128)(2,1)S(1)}, u32[]{:S(2)}, u32[]{:S(2)}) collective-permute-start(bf16[2,128,384]{2,1,0:T(8,128)(2,1)S(1)} %get-tuple-element.61), channel_id=1, source_target_pairs={{0,8},{1,3},{16,24},{17,19},{32,40},{33,35},{48,56},{49,51},{64,72... | collective-permute-start | bytes 589832 | tf_op jit(solution)/shard_map/gather/ppermute | solution.py:31
  5.4 6.0 %collective-permute-start = (bf16[2,128,384]{2,1,0:T(8,128)(2,1)S(1)}, bf16[2,128,384]{2,1,0:T(8,128)(2,1)S(1)}, u32[]{:S(2)}, u32[]{:S(2)}) collective-permute-start(bf16[2,128,384]{2,1,0:T(8,128)(2,1)S(1)} %get-tuple-element.61), channel_id=1, source_target_pairs={{0,4},{1,129},{16,20},{17,145},{32,36},{33,161},{48,52},{49,177},{... | collective-permute-start | bytes 589832 | tf_op jit(solution)/shard_map/gather/ppermute | solution.py:31
  5.8 5.6 %collective-permute-start.2 = (bf16[2,128,384]{2,1,0:T(8,128)(2,1)S(1)}, bf16[2,128,384]{2,1,0:T(8,128)(2,1)S(1)}, u32[]{:S(2)}, u32[]{:S(2)}) collective-permute-start(bf16[2,128,384]{2,1,0:T(8,128)(2,1)S(1)} %get-tuple-element.61), channel_id=1, source_target_pairs={{0,12},{1,131},{16,28},{17,147},{32,44},{33,163},{48,60},{49,179},... | collective-permute-start | bytes 589832 | tf_op jit(solution)/shard_map/gather/ppermute | solution.py:31
  11.6 12.8 %collective-permute-start.5 = (bf16[4,2,128,384]{3,2,1,0:T(8,128)(2,1)S(1)}, bf16[4,2,128,384]{3,2,1,0:T(8,128)(2,1)S(1)}, u32[]{:S(2)}, u32[]{:S(2)}) collective-permute-start(bf16[4,2,128,384]{3,2,1,0:T(8,128)(2,1)S(1)} %pad_maximum_fusion.refs_0_), channel_id=1, source_target_pairs={{0,2},{1,9},{16,18},{17,25},{32,34},{33,41},{48,50},{49,57},{64,66... | collective-permute-start | bytes 2359304 | tf_op jit(solution)/shard_map/gather/ppermute | solution.py:31
  14.3 18.6 %collective-permute-start.4 = (bf16[4,2,128,384]{3,2,1,0:T(8,128)(2,1)S(1)}, bf16[4,2,128,384]{3,2,1,0:T(8,128)(2,1)S(1)}, u32[]{:S(2)}, u32[]{:S(2)}) collective-permute-start(bf16[4,2,128,384]{3,2,1,0:T(8,128)(2,1)S(1)} %pad_maximum_fusion.refs_0_), channel_id=1, source_target_pairs={{0,130},{1,13},{16,146},{17,29},{32,162},{33,45},{48,178},{49,61},... | collective-permute-start | bytes 2359304 | tf_op jit(solution)/shard_map/gather/ppermute | solution.py:31
  15.1 20.5 %collective-permute-start.3 = (bf16[4,2,128,384]{3,2,1,0:T(8,128)(2,1)S(1)}, bf16[4,2,128,384]{3,2,1,0:T(8,128)(2,1)S(1)}, u32[]{:S(2)}, u32[]{:S(2)}) collective-permute-start(bf16[4,2,128,384]{3,2,1,0:T(8,128)(2,1)S(1)} %pad_maximum_fusion.refs_0_), channel_id=1, source_target_pairs={{0,128},{1,5},{16,144},{17,21},{32,160},{33,37},{48,176},{49,53},{... | collective-permute-start | bytes 2359304 | tf_op jit(solution)/shard_map/gather/ppermute | solution.py:31
  15.7 22.3 %collective-permute-start.6 = (bf16[4,2,128,384]{3,2,1,0:T(8,128)(2,1)S(1)}, bf16[4,2,128,384]{3,2,1,0:T(8,128)(2,1)}, u32[]{:S(2)}, u32[]{:S(2)}) collective-permute-start(bf16[4,2,128,384]{3,2,1,0:T(8,128)(2,1)S(1)} %pad_maximum_fusion.refs_0_), channel_id=1, source_target_pairs={{0,1},{1,0},{16,17},{17,16},{32,33},{33,32},{48,49},{49,48},{64,65... | collective-permute-start | bytes 2359304 | tf_op jit(solution)/shard_map/gather/ppermute | solution.py:31
  24.4 13.7 %collective-permute-start.9 = (bf16[4,2,128,384]{3,2,1,0:T(8,128)(2,1)S(1)}, bf16[4,2,128,384]{3,2,1,0:T(8,128)(2,1)}, u32[]{:S(2)}, u32[]{:S(2)}) collective-permute-start(bf16[4,2,128,384]{3,2,1,0:T(8,128)(2,1)S(1)} %collective-permute-done.5.refs_3_), channel_id=1, source_target_pairs={{0,1},{1,0},{16,17},{17,16},{32,33},{33,32},{48,49},{49,48},{64,65... | collective-permute-start | bytes 2359304 | tf_op jit(solution)/shard_map/gather/ppermute | solution.py:31
  32.9 5.2 %collective-permute-start.8 = (bf16[4,2,128,384]{3,2,1,0:T(8,128)(2,1)S(1)}, bf16[4,2,128,384]{3,2,1,0:T(8,128)(2,1)}, u32[]{:S(2)}, u32[]{:S(2)}) collective-permute-start(bf16[4,2,128,384]{3,2,1,0:T(8,128)(2,1)S(1)} %collective-permute-done.4.refs_2_), channel_id=1, source_target_pairs={{0,1},{1,0},{16,17},{17,16},{32,33},{33,32},{48,49},{49,48},{64,65... | collective-permute-start | bytes 2359304 | tf_op jit(solution)/shard_map/gather/ppermute | solution.py:31
  35.6 3.2 %collective-permute-start.7 = (bf16[4,2,128,384]{3,2,1,0:T(8,128)(2,1)S(1)}, bf16[4,2,128,384]{3,2,1,0:T(8,128)(2,1)}, u32[]{:S(2)}, u32[]{:S(2)}) collective-permute-start(bf16[4,2,128,384]{3,2,1,0:T(8,128)(2,1)S(1)} %collective-permute-done.3.refs_1_), channel_id=1, source_target_pairs={{0,1},{1,0},{16,17},{17,16},{32,33},{33,32},{48,49},{49,48},{64,65... | collective-permute-start | bytes 2359304 | tf_op jit(solution)/shard_map/gather/ppermute | solution.py:31
  38.8 1.9 %copy-start = (bf16[6,4,256,256]{3,2,1,0:T(8,128)(2,1)S(1)}, bf16[6,4,256,256]{3,2,1,0:T(8,128)(2,1)}, u32[]{:S(2)}) copy-start(bf16[6,4,256,256]{3,2,1,0:T(8,128)(2,1)} %up_ref.1) | copy-start | bytes 9437188
  40.7 6.9 %copy-start.1 = (bf16[6,4,256,256]{3,2,1,0:T(8,128)(2,1)S(1)}, bf16[6,4,256,256]{3,2,1,0:T(8,128)(2,1)}, u32[]{:S(2)}) copy-start(bf16[6,4,256,256]{3,2,1,0:T(8,128)(2,1)} %up_ref.1) | copy-start | bytes 9437188
  40.7 6.9 %copy-start.2 = (bf16[6,4,256,256]{3,2,1,0:T(8,128)(2,1)S(1)}, bf16[6,4,256,256]{3,2,1,0:T(8,128)(2,1)}, u32[]{:S(2)}) copy-start(bf16[6,4,256,256]{3,2,1,0:T(8,128)(2,1)} %down_ref.1) | copy-start | bytes 9437188
  50.8 10.9 %collective-permute-start.10 = (bf16[2,2,2,128,384]{4,3,2,1,0:T(8,128)(2,1)S(1)}, bf16[2,2,2,128,384]{4,3,2,1,0:T(8,128)(2,1)S(1)}, u32[]{:S(2)}, u32[]{:S(2)}) collective-permute-start(bf16[2,2,2,128,384]{4,3,2,1,0:T(8,128)(2,1)S(1)} %get-tuple-element.30), channel_id=1, source_target_pairs={{0,1},{1,0},{16,17},{17,16},{32,33},{33,32},{48,49},{49,48},{64,65... | collective-permute-start | bytes 2359304 | tf_op jit(solution)/shard_map/scatter/ppermute | solution.py:31
  51.2 10.3 %collective-permute-start.12 = (bf16[2,24,16,256]{3,2,1,0:T(8,128)(2,1)S(1)}, bf16[2,24,16,256]{3,2,1,0:T(8,128)(2,1)S(1)}, u32[]{:S(2)}, u32[]{:S(2)}) collective-permute-start(bf16[2,24,16,256]{3,2,1,0:T(8,128)(2,1)S(1)} %get-tuple-element.36), channel_id=1, source_target_pairs={{0,16},{1,113},{16,32},{17,1},{32,48},{33,17},{48,64},{49,33},{64,... | collective-permute-start | bytes 1179656 | tf_op jit(solution)/shard_map/weight_sums/ppermute | solution.py:31
  56.8 5.0 %collective-permute-start.11 = (bf16[2,2,2,128,384]{4,3,2,1,0:T(8,128)(2,1)S(1)}, bf16[2,2,2,128,384]{4,3,2,1,0:T(8,128)(2,1)S(1)}, u32[]{:S(2)}, u32[]{:S(2)}) collective-permute-start(bf16[2,2,2,128,384]{4,3,2,1,0:T(8,128)(2,1)S(1)} %get-tuple-element.32), channel_id=1, source_target_pairs={{0,1},{1,0},{16,17},{17,16},{32,33},{33,32},{48,49},{49,48},{64,65... | collective-permute-start | bytes 2359304 | tf_op jit(solution)/shard_map/scatter/ppermute | solution.py:31
  62.0 10.3 %collective-permute-start.16 = (bf16[2,24,16,256]{3,2,1,0:T(8,128)(2,1)S(1)}, bf16[2,24,16,256]{3,2,1,0:T(8,128)(2,1)S(1)}, u32[]{:S(2)}, u32[]{:S(2)}) collective-permute-start(bf16[2,24,16,256]{3,2,1,0:T(8,128)(2,1)S(1)} %fusion.6), channel_id=1, source_target_pairs={{0,16},{1,113},{16,32},{17,1},{32,48},{33,17},{48,64},{49,33},{64,... | collective-permute-start | bytes 1179656 | tf_op jit(solution)/shard_map/weight_sums/ppermute | solution.py:31
  65.2 11.1 %collective-permute-start.17 = (bf16[2,24,16,256]{3,2,1,0:T(8,128)(2,1)S(1)}, bf16[2,24,16,256]{3,2,1,0:T(8,128)(2,1)S(1)}, u32[]{:S(2)}, u32[]{:S(2)}) collective-permute-start(bf16[2,24,16,256]{3,2,1,0:T(8,128)(2,1)S(1)} %slice_bitcast_fusion.4), channel_id=1, source_target_pairs={{0,112},{1,17},{16,0},{17,33},{32,16},{33,49},{48,32},{49,65},{64,... | collective-permute-start | bytes 1179656 | tf_op jit(solution)/shard_map/weight_sums/ppermute | solution.py:31
  65.2 13.1 %collective-permute-start.13 = (bf16[2,2,128,384]{3,2,1,0:T(8,128)(2,1)S(1)}, bf16[2,2,128,384]{3,2,1,0:T(8,128)(2,1)S(1)}, u32[]{:S(2)}, u32[]{:S(2)}) collective-permute-start(bf16[2,2,128,384]{3,2,1,0:T(8,128)(2,1)S(1)} %get-tuple-element.37), channel_id=1, source_target_pairs={{0,4},{1,5},{16,20},{17,21},{32,36},{33,37},{48,52},{49,53},{64,68... | collective-permute-start | bytes 1179656 | tf_op jit(solution)/shard_map/scatter/ppermute | solution.py:31
  65.8 19.5 %collective-permute-start.14 = (bf16[2,2,128,384]{3,2,1,0:T(8,128)(2,1)S(1)}, bf16[2,2,128,384]{3,2,1,0:T(8,128)(2,1)S(1)}, u32[]{:S(2)}, u32[]{:S(2)}) collective-permute-start(bf16[2,2,128,384]{3,2,1,0:T(8,128)(2,1)S(1)} %get-tuple-element.38), channel_id=1, source_target_pairs={{0,8},{1,9},{16,24},{17,25},{32,40},{33,41},{48,56},{49,57},{64,72... | collective-permute-start | bytes 1179656 | tf_op jit(solution)/shard_map/scatter/ppermute | solution.py:31
  69.3 16.4 %collective-permute-start.15 = (bf16[2,2,128,384]{3,2,1,0:T(8,128)(2,1)S(1)}, bf16[2,2,128,384]{3,2,1,0:T(8,128)(2,1)S(1)}, u32[]{:S(2)}, u32[]{:S(2)}) collective-permute-start(bf16[2,2,128,384]{3,2,1,0:T(8,128)(2,1)S(1)} %fusion.7), channel_id=1, source_target_pairs={{0,12},{1,13},{16,28},{17,29},{32,44},{33,45},{48,60},{49,61},{64,... | collective-permute-start | bytes 1179656 | tf_op jit(solution)/shard_map/scatter/ppermute | solution.py:31
  76.5 11.2 %collective-permute-start.19 = (bf16[2,24,16,256]{3,2,1,0:T(8,128)(2,1)S(1)}, bf16[2,24,16,256]{3,2,1,0:T(8,128)(2,1)S(1)}, u32[]{:S(2)}, u32[]{:S(2)}) collective-permute-start(bf16[2,24,16,256]{3,2,1,0:T(8,128)(2,1)S(1)} %get-tuple-element.42), channel_id=1, source_target_pairs={{0,16},{1,113},{16,32},{17,1},{32,48},{33,17},{48,64},{49,33},{64,... | collective-permute-start | bytes 1179656 | tf_op jit(solution)/shard_map/weight_sums/ppermute | solution.py:31
  76.8 11.7 %collective-permute-start.20 = (bf16[2,24,16,256]{3,2,1,0:T(8,128)(2,1)S(1)}, bf16[2,24,16,256]{3,2,1,0:T(8,128)(2,1)S(1)}, u32[]{:S(2)}, u32[]{:S(2)}) collective-permute-start(bf16[2,24,16,256]{3,2,1,0:T(8,128)(2,1)S(1)} %get-tuple-element.43), channel_id=1, source_target_pairs={{0,112},{1,17},{16,0},{17,33},{32,16},{33,49},{48,32},{49,65},{64,... | collective-permute-start | bytes 1179656 | tf_op jit(solution)/shard_map/weight_sums/ppermute | solution.py:31
  86.0 6.1 %collective-permute-start.18 = (bf16[2,128,384]{2,1,0:T(8,128)(2,1)S(1)}, bf16[2,128,384]{2,1,0:T(8,128)(2,1)S(1)}, u32[]{:S(2)}, u32[]{:S(2)}) collective-permute-start(bf16[2,128,384]{2,1,0:T(8,128)(2,1)S(1)} %slice_bitcast_fusion.5), channel_id=1, source_target_pairs={{0,2},{1,3},{16,18},{17,19},{32,34},{33,35},{48,50},{49,51},{64,66... | collective-permute-start | bytes 589832 | tf_op jit(solution)/shard_map/scatter/ppermute | solution.py:31
  88.7 10.6 %collective-permute-start.21 = (bf16[2,24,16,256]{3,2,1,0:T(8,128)(2,1)S(1)}, bf16[2,24,16,256]{3,2,1,0:T(8,128)(2,1)S(1)}, u32[]{:S(2)}, u32[]{:S(2)}) collective-permute-start(bf16[2,24,16,256]{3,2,1,0:T(8,128)(2,1)S(1)} %get-tuple-element.47), channel_id=1, source_target_pairs={{0,16},{1,113},{16,32},{17,1},{32,48},{33,17},{48,64},{49,33},{64,... | collective-permute-start | bytes 1179656 | tf_op jit(solution)/shard_map/weight_sums/ppermute | solution.py:31
  92.1 10.8 %collective-permute-start.22 = (bf16[2,24,16,256]{3,2,1,0:T(8,128)(2,1)S(1)}, bf16[2,24,16,256]{3,2,1,0:T(8,128)(2,1)S(1)}, u32[]{:S(2)}, u32[]{:S(2)}) collective-permute-start(bf16[2,24,16,256]{3,2,1,0:T(8,128)(2,1)S(1)} %get-tuple-element.48), channel_id=1, source_target_pairs={{0,112},{1,17},{16,0},{17,33},{32,16},{33,49},{48,32},{49,65},{64,... | collective-permute-start | bytes 1179656 | tf_op jit(solution)/shard_map/weight_sums/ppermute | solution.py:31

commit v3 on v2

v3 whole, which is shorter than its diff:
```python
import jax
import jax.numpy as jnp
from jax import lax
from jax.experimental import pallas as pl
from jax.experimental.pallas import tpu as pltpu
from jax.sharding import Mesh, PartitionSpec as P

BLK = 256
HALF = 128
WIDE = 384
K = 4
NH = 6
NB = NH * K
AXES = ("ylo", "z", "x", "yhi", "core")
VMEM_LIMIT = 40 * 1024 * 1024
BF16, F32 = jnp.bfloat16, jnp.float32


def device_id(x, y, z, c):
    return ((y % 2) * 8 + z) * 16 + x * 4 + (y // 2) * 2 + c


def permute(value, target):
    pairs = []
    for x in range(4):
        for y in range(4):
            for z in range(8):
                for c in range(2):
                    tx, ty, tz, tc = target(x, y, z, c)
                    pairs.append((device_id(x, y, z, c), device_id(tx % 4, ty % 4, tz % 8, tc)))
    return lax.ppermute(value, AXES, pairs)


def other_core(x, y, z, c):
    return x, y, z, 1 - c


def ahead_z(x, y, z, c):
    return x, y, (z + 1 if c == 0 else z - 1), c


def back_z(x, y, z, c):
    return x, y, (z - 1 if c == 0 else z + 1), c


def gather_first(step):
    return lambda x, y, z, c: (x + step, y, z, c) if c == 0 else (x, y + step, z, c)


def gather_second(step):
    return lambda x, y, z, c: (x, y + step, z, c) if c == 0 else (x + step, y, z, c)


def along_x(step):
    return lambda x, y, z, c: (x + step, y, z, c)


def across_y(x, y, z, c):
    return x, y + 2, z, c


def place():
    return [lax.axis_index(a) for a in AXES]


def unit_owner(unit):
    return (unit * 43) >> 7


def gathered_quarter(all_ref, kind, unit, token_half, x, y, core):
    t = unit_owner(unit)
    lane = (unit - 3 * t) * HALF
    c = t & 1
    dx = (x - (t >> 2)) & 3
    dy = (y - ((t & 2) + token_half)) & 3
    first = jnp.where(c == 0, dx, dy)
    second = jnp.where(c == 0, dy, dx)
    return all_ref[kind, c ^ core, second, first, :, pl.ds(pl.multiple_of(lane, HALF), HALF)]


def gathered_block(all_ref, kind, b, x, y, core):
    rows = []
    for h in range(2):
        cols = [gathered_quarter(all_ref, kind, 2 * b + u, h, x, y, core) for u in range(2)]
        rows.append(jnp.concatenate(cols, axis=1))
    return jnp.concatenate(rows, axis=0)


def dot(a, b, a_dim, b_dim):
    return lax.dot_general(a, b, (((a_dim,), (b_dim,)), ((), ())), preferred_element_type=F32)


def grads_kernel(index, *refs):
    parts, (up_hbm, down_hbm) = refs[0:8], refs[8:10]
    dw_ref, far_ref, keep, give = *refs[10:12], refs[12:16], refs[16:18]
    hid_ref, acc_ref, all_ref, up_ref, down_ref, pre_ref, sem = refs[18:]
    ylo, z, x, yhi, core = place()
    y = yhi * 2 + ylo

    def fetch(kind):
        for slot in range(2):
            for i, e in enumerate((0, 1, 3, 2)):
                pltpu.make_async_copy(
                    parts[4 * slot + i].at[:, kind], all_ref.at[kind, slot, e], sem.at[kind]
                ).start()

    def await_all(ref, i):
        pltpu.make_async_copy(ref, ref, sem.at[i]).wait()

    fetch(0)
    up_copy = pltpu.make_async_copy(up_hbm, up_ref, sem.at[2])
    up_copy.start()
    fetch(1)
    down_copy = pltpu.make_async_copy(down_hbm, down_ref, sem.at[3])
    down_copy.start()

    def store_rows(g, j, value):
        value = value.astype(BF16)
        for i in range(8):
            r = jnp.where(core == 0, i - z, z - i) & 7
            dw_ref[r, g, j] = value[i * 16 : i * 16 + 16]

    def add(kind, b, value):
        for u in range(2):
            unit = 2 * b + u
            t = unit_owner(unit)
            lane = (unit - 3 * t) * HALF
            dx = ((t >> 2) - x) & 3
            dy = ((t >> 1) & 1) ^ yhi
            where = ((((t & 1) ^ core) * 4 + dx) * 2 + dy) * 2 + kind
            acc_ref[where, :, pl.ds(pl.multiple_of(lane, HALF), HALF)] += value[
                :, u * HALF : (u + 1) * HALF
            ]

    acc_ref[...] = jnp.zeros_like(acc_ref)
    own = pl.ds(pl.multiple_of(ylo * HALF, HALF), HALF)
    await_all(all_ref.at[0], 0)
    up_copy.wait()
    for n in range(NH):
        acc = jnp.zeros((BLK, BLK), F32)
        for k in range(K):
            tok = gathered_block(all_ref, 0, index[0, k, n], x, y, core)
            acc += dot(tok, up_ref[n, k], 1, 0)
        pre_ref[n] = acc
        hid_ref[n] = (acc * jax.nn.sigmoid(acc)).astype(BF16)
    await_all(all_ref.at[1], 1)
    down_copy.wait()
    for n in range(NH):
        hidden, my_hidden = hid_ref[n, :, own], hid_ref[n, own]
        acc = jnp.zeros((BLK, BLK), F32)
        for k in range(K):
            cot = gathered_block(all_ref, 1, index[1, k, n], x, y, core)
            acc += dot(cot, down_ref[n, k], 1, 1)
            store_rows(1, n * K + k, dot(hidden, cot, 0, 0))
            add(0, index[1, k, n], dot(my_hidden, down_ref[n, k], 1, 0))
        pre = pre_ref[n]
        sig = jax.nn.sigmoid(pre)
        pre_grad = (acc * (sig * (1.0 + pre * (1.0 - sig)))).astype(BF16)
        hid_ref[n] = pre_grad
        my_grad = hid_ref[n, own]
        toks = []
        for k in range(K):
            unit = 2 * index[0, k, n] + ylo
            halves = [gathered_quarter(all_ref, 0, unit, h, x, y, core) for h in range(2)]
            toks.append(jnp.concatenate(halves, axis=0))
            add(1, index[0, k, n], dot(my_grad, up_ref[n, k], 1, 1))
        grads = dot(jnp.concatenate(toks, axis=1), pre_grad, 0, 0)
        for k in range(K):
            store_rows(0, n * K + k, grads[k * HALF : (k + 1) * HALF])
    far_ref[...] = dw_ref[4]
    for dx in range(4):
        for dy in range(2):
            for kind in range(2):
                keep[dx][dy, kind] = acc_ref[(dx * 2 + dy) * 2 + kind].astype(BF16)
                other = acc_ref[((4 + dx) * 2 + dy) * 2 + kind].astype(BF16)
                give[0 if dx in (1, 2) else 1][dx // 2, dy, kind] = other


def specs(space, count):
    return [pl.BlockSpec(memory_space=space)] * count


def run(kernel, name, args, in_specs, out_shape, scratch, flops, moved):
    return pl.pallas_call(
        kernel,
        out_shape=tuple(out_shape),
        in_specs=in_specs,
        out_specs=tuple(specs(pltpu.VMEM, len(out_shape))),
        scratch_shapes=scratch,
        compiler_params=pltpu.CompilerParams(vmem_limit_bytes=VMEM_LIMIT),
        cost_estimate=pl.CostEstimate(flops=flops, bytes_accessed=moved, transcendentals=0),
        name=name,
    )(*args)


def shape(*dims, dtype=BF16):
    return jax.ShapeDtypeStruct(dims, dtype)


def wide_sum(*terms):
    total = terms[0].astype(F32)
    for term in terms[1:]:
        total = total + term.astype(F32)
    return total.astype(BF16)


def on_device(tokens, cotangent, up_blocks, up_index, down_blocks, down_index):

    tie = lax.optimization_barrier
    with jax.named_scope("gather"):
        own = jnp.stack([tokens, cotangent])
        line = [permute(own, gather_first(d)) for d in (3, 1, 2)]
        *line, up_index, down_index = tie((*line, up_index, down_index))
        index = jnp.stack([up_index.T, down_index.T])
        line = jnp.stack([own, line[1], line[2], line[0]])
        mine = [line] + [permute(line, gather_second(e)) for e in (1, 3, 2)]
        theirs = [permute(part, other_core) for part in mine]

    piece = HALF * WIDE * 2
    matmul = 2 * BLK**3
    smem, vmem, anyw = pltpu.SMEM, pltpu.VMEM, pl.ANY
    parts, far, *rest = run(
        grads_kernel,
        "grads",
        (index, *mine, *theirs, up_blocks, down_blocks),
        specs(smem, 1) + specs(anyw, 10),
        [shape(8, 2, NB, 16, BLK)]
        + [shape(2, NB, 16, BLK)]
        + [shape(2, 2, HALF, WIDE)] * 4
        + [shape(2, 2, 2, HALF, WIDE)] * 2,
        [
            pltpu.VMEM((NH, BLK, BLK), BF16),
            pltpu.VMEM((32, HALF, WIDE), F32),
            pltpu.VMEM((2, 2, 4, 4, HALF, WIDE), BF16),
            pltpu.VMEM((NH, K, BLK, BLK), BF16),
            pltpu.VMEM((NH, K, BLK, BLK), BF16),
            pltpu.VMEM((NH, BLK, BLK), F32),
            pltpu.SemaphoreType.DMA((4,)),
        ],
        96 * matmul,
        128 * piece,
    )
    keep, (give_a, give_b) = rest[:4], rest[4:]
    ahead = permute(far, ahead_z)
    got_a, got_b = permute(give_a, other_core), permute(give_b, other_core)
    sums = [wide_sum(keep[dx], got) for dx, got in ((1, got_a[0]), (2, got_a[1]), (3, got_b[1]))]
    *sums, ahead, back = tie((*sums, wide_sum(parts[3], ahead), parts[5]))
    ahead, back = permute(ahead, ahead_z), permute(back, back_z)
    sent = [permute(total, along_x(dx)) for dx, total in zip((1, 2, 3), sums)]
    ahead, back = tie((wide_sum(parts[2], ahead), wide_sum(parts[6], back)))
    *sent, _, _ = tie((*sent, ahead, back))
    ahead, back = permute(ahead, ahead_z), permute(back, back_z)
    line_sum = wide_sum(keep[0], got_b[0], *sent)
    across = permute(line_sum[1], across_y)
    ahead, back = tie((wide_sum(parts[1], ahead), wide_sum(parts[7], back)))
    across, _, _ = tie((across, ahead, back))
    ahead, back = permute(ahead, ahead_z), permute(back, back_z)
    final = wide_sum(line_sum[0], across)
    weight_grads = wide_sum(parts[0], ahead, back)

    rows = (NH, K, 16, BLK)
    return final[0], final[1], weight_grads[0].reshape(rows), weight_grads[1].reshape(rows)


def solution(mesh):
    fine = Mesh(mesh.devices.reshape(2, 8, 4, 2, 2), AXES)
    dp, tensor = ("ylo", "z"), ("x", "yhi", "core")
    in_specs = (
        P(dp, tensor),
        P(dp, tensor),
        P(tensor, None, None, None),
        P(tensor, None),
        P(tensor, None, None, None),
        P(tensor, None),
    )
    out_specs = (
        P(dp, tensor),
        P(dp, tensor),
        P(tensor, None, dp, None),
        P(tensor, None, dp, None),
    )
    return jax.shard_map(
        on_device, mesh=fine, in_specs=in_specs, out_specs=out_specs, check_vma=False
    )
```

time: 104 us -> 101 us (0.971)
  local copies, waits for them, and re-layouts: 5.1 us -> 1.51 us
  Pallas kernels: 10 us -> 8.71 us
    unnamed x8 -> x0, local copies, waits for them, and re-layouts: 3.43 us -> none
    pallas_call x2 -> x1, Pallas kernels: 10 us -> 8.71 us  [run(): pl.pallas_call(kernel, out_shape=tuple(out_shape), in_specs=in_specs, out...]
  transfers between devices with their start and end apart: 23 -> 23, of which waited for: 14 -> 15; matrix products, arithmetic and copies ran while one was open for 3% -> 2% of each run, Pallas kernels for 0% -> 0%
where the time goes in v3:
time: 101 us; the launch traced here: 100 us
  waiting for transfers between devices  45.5 us (45%)
  starting transfers between devices  40.8 us (40%)
  Pallas kernels  8.71 us (9%)
  other arithmetic  3.19 us (3%)
  local copies, waits for them, and re-layouts  1.51 us (1%)
    ppermute x23, waiting for transfers between devices, permute(): return lax.ppermute(value, AXES, pairs)  45.5 us
    ppermute x23, starting transfers between devices, permute(): return lax.ppermute(value, AXES, pairs)  40.8 us
    pallas_call x1, Pallas kernels, run(): pl.pallas_call(kernel, out_shape=tuple(out_shape), in_specs=in_specs, out...  8.71 us
  transfers between devices with their start and end apart: 23, of which 15 were waited for; matrix products, arithmetic and copies ran while one was open for 2% of the time, Pallas kernels for 0%

profile of v3, /device:TPU:1, one launch (start us, length us, event | category | flops | bytes accessed | tf_op | source)
XLA Modules:
  0.0 100.4 jit_solution(2481683034343087923)
XLA Ops:
  0.6 1.0 fusion.15
  1.6 3.8 %collective-permute-start.2 = (bf16[2,128,384]{2,1,0:T(8,128)(2,1)S(1)}, bf16[2,128,384]{2,1,0:T(8,128)(2,1)S(1)}, u32[]{:S(2)}, u32[]{:S(2)}) collective-permute-start(bf16[2,128,384]{2,1,0:T(8,128)(2,1)S(1)} %get-tuple-element.67), channel_id=1, source_target_pairs={{0,8},{1,3},{16,24},{17,19},{32,40},{33,35},{48,56},{49,51},{64,72... | collective-permute-start | bytes 589832 | tf_op jit(solution)/shard_map/gather/ppermute | solution.py:31
  5.4 0.4 collective-permute-start.1
  5.8 2.3 %collective-permute-start = (bf16[2,128,384]{2,1,0:T(8,128)(2,1)S(1)}, bf16[2,128,384]{2,1,0:T(8,128)(2,1)S(1)}, u32[]{:S(2)}, u32[]{:S(2)}) collective-permute-start(bf16[2,128,384]{2,1,0:T(8,128)(2,1)S(1)} %get-tuple-element.67), channel_id=1, source_target_pairs={{0,12},{1,131},{16,28},{17,147},{32,44},{33,163},{48,60},{49,179},... | collective-permute-start | bytes 589832 | tf_op jit(solution)/shard_map/gather/ppermute | solution.py:31
  8.1 0.4 collective-permute-done.2
  8.5 3.0 %collective-permute-done.1 = bf16[2,128,384]{2,1,0:T(8,128)(2,1)S(1)} collective-permute-done((bf16[2,128,384]{2,1,0:T(8,128)(2,1)S(1)}, bf16[2,128,384]{2,1,0:T(8,128)(2,1)S(1)}, u32[]{:S(2)}, u32[]{:S(2)}) %collective-permute-start.1) | collective-permute-done | bytes 196640 | tf_op jit(solution)/shard_map/gather/ppermute | solution.py:31
  11.5 0.1 pad_maximum_fusion.refs_0_
  11.6 2.7 %collective-permute-start.5 = (bf16[4,2,128,384]{3,2,1,0:T(8,128)(2,1)S(1)}, bf16[4,2,128,384]{3,2,1,0:T(8,128)(2,1)S(1)}, u32[]{:S(2)}, u32[]{:S(2)}) collective-permute-start(bf16[4,2,128,384]{3,2,1,0:T(8,128)(2,1)S(1)} %pad_maximum_fusion.refs_0_), channel_id=1, source_target_pairs={{0,2},{1,9},{16,18},{17,25},{32,34},{33,41},{48,50},{49,57},{64,66... | collective-permute-start | bytes 2359304 | tf_op jit(solution)/shard_map/gather/ppermute | solution.py:31
  14.3 0.9 collective-permute-start.4
  15.1 0.6 collective-permute-start.3
  15.7 2.8 %collective-permute-start.6 = (bf16[4,2,128,384]{3,2,1,0:T(8,128)(2,1)S(1)}, bf16[4,2,128,384]{3,2,1,0:T(8,128)(2,1)S(1)}, u32[]{:S(2)}, u32[]{:S(2)}) collective-permute-start(bf16[4,2,128,384]{3,2,1,0:T(8,128)(2,1)S(1)} %pad_maximum_fusion.refs_0_), channel_id=1, source_target_pairs={{0,1},{1,0},{16,17},{17,16},{32,33},{33,32},{48,49},{49,48},{64,65... | collective-permute-start | bytes 2359304 | tf_op jit(solution)/shard_map/gather/ppermute | solution.py:31
  18.5 5.8 %collective-permute-done.5.refs_3_ = bf16[4,2,128,384]{3,2,1,0:T(8,128)(2,1)S(1)} collective-permute-done((bf16[4,2,128,384]{3,2,1,0:T(8,128)(2,1)S(1)}, bf16[4,2,128,384]{3,2,1,0:T(8,128)(2,1)S(1)}, u32[]{:S(2)}, u32[]{:S(2)}) %collective-permute-start.5) | collective-permute-done | bytes 786464 | tf_op jit(solution)/shard_map/gather/ppermute | solution.py:31
  24.4 3.7 %collective-permute-start.9 = (bf16[4,2,128,384]{3,2,1,0:T(8,128)(2,1)S(1)}, bf16[4,2,128,384]{3,2,1,0:T(8,128)(2,1)S(1)}, u32[]{:S(2)}, u32[]{:S(2)}) collective-permute-start(bf16[4,2,128,384]{3,2,1,0:T(8,128)(2,1)S(1)} %collective-permute-done.5.refs_3_), channel_id=1, source_target_pairs={{0,1},{1,0},{16,17},{17,16},{32,33},{33,32},{48,49},{49,48},{64,65... | collective-permute-start | bytes 2359304 | tf_op jit(solution)/shard_map/gather/ppermute | solution.py:31
  28.0 4.8 %collective-permute-done.4.refs_2_ = bf16[4,2,128,384]{3,2,1,0:T(8,128)(2,1)S(1)} collective-permute-done((bf16[4,2,128,384]{3,2,1,0:T(8,128)(2,1)S(1)}, bf16[4,2,128,384]{3,2,1,0:T(8,128)(2,1)S(1)}, u32[]{:S(2)}, u32[]{:S(2)}) %collective-permute-start.4) | collective-permute-done | bytes 786464 | tf_op jit(solution)/shard_map/gather/ppermute | solution.py:31
  32.9 2.8 %collective-permute-start.8 = (bf16[4,2,128,384]{3,2,1,0:T(8,128)(2,1)S(1)}, bf16[4,2,128,384]{3,2,1,0:T(8,128)(2,1)S(1)}, u32[]{:S(2)}, u32[]{:S(2)}) collective-permute-start(bf16[4,2,128,384]{3,2,1,0:T(8,128)(2,1)S(1)} %collective-permute-done.4.refs_2_), channel_id=1, source_target_pairs={{0,1},{1,0},{16,17},{17,16},{32,33},{33,32},{48,49},{49,48},{64,65... | collective-permute-start | bytes 2359304 | tf_op jit(solution)/shard_map/gather/ppermute | solution.py:31
  35.6 0.7 collective-permute-start.7
  36.4 0.7 pad_add_fusion.index
  37.1 0.5 collective-permute-done.8.refs_6_
  37.5 1.1 %collective-permute-done.7.refs_5_ = bf16[4,2,128,384]{3,2,1,0:T(8,128)(2,1)S(1)} collective-permute-done((bf16[4,2,128,384]{3,2,1,0:T(8,128)(2,1)S(1)}, bf16[4,2,128,384]{3,2,1,0:T(8,128)(2,1)S(1)}, u32[]{:S(2)}, u32[]{:S(2)}) %collective-permute-start.7) | collective-permute-done | bytes 786464 | tf_op jit(solution)/shard_map/gather/ppermute | solution.py:31
  38.7 8.7 %grads.1 = (bf16[8,2,24,16,256]{4,3,2,1,0:T(8,128)(2,1)S(1)}, bf16[2,24,16,256]{3,2,1,0:T(8,128)(2,1)S(1)}, bf16[2,2,128,384]{3,2,1,0:T(8,128)(2,1)S(1)}, bf16[2...) custom-call(s32[2,4,6]{2,1,0:T(4,128)S(1)} %pad_add_fusion.index, ...), custom_call_target="tpu_custom_call" | custom-call | flops 3221225472 | bytes 12582912 | tf_op jit(solution)/shard_map/grads/pallas_call | solution.py:184
  47.4 0.5 collective-permute-start.10
  47.9 5.6 %collective-permute-start.12 = (bf16[2,24,16,256]{3,2,1,0:T(8,128)(2,1)S(1)}, bf16[2,24,16,256]{3,2,1,0:T(8,128)(2,1)S(1)}, u32[]{:S(2)}, u32[]{:S(2)}) collective-permute-start(bf16[2,24,16,256]{3,2,1,0:T(8,128)(2,1)S(1)} %get-tuple-element.42), channel_id=1, source_target_pairs={{0,16},{1,113},{16,32},{17,1},{32,48},{33,17},{48,64},{49,33},{64,... | collective-permute-start | bytes 1179656 | tf_op jit(solution)/shard_map/ppermute | solution.py:31
  53.5 4.7 %collective-permute-done.12 = bf16[2,24,16,256]{3,2,1,0:T(8,128)(2,1)S(1)} collective-permute-done((bf16[2,24,16,256]{3,2,1,0:T(8,128)(2,1)S(1)}, bf16[2,24,16,256]{3,2,1,0:T(8,128)(2,1)S(1)}, u32[]{:S(2)}, u32[]{:S(2)}) %collective-permute-start.12) | collective-permute-done | bytes 393248 | tf_op jit(solution)/shard_map/ppermute | solution.py:31
  58.1 0.1 fusion.6
  58.3 0.1 fusion.7
  58.4 0.2 fusion.8
  58.6 3.2 %collective-permute-start.16 = (bf16[2,24,16,256]{3,2,1,0:T(8,128)(2,1)S(1)}, bf16[2,24,16,256]{3,2,1,0:T(8,128)(2,1)S(1)}, u32[]{:S(2)}, u32[]{:S(2)}) collective-permute-start(bf16[2,24,16,256]{3,2,1,0:T(8,128)(2,1)S(1)} %fusion.6), channel_id=1, source_target_pairs={{0,16},{1,113},{16,32},{17,1},{32,48},{33,17},{48,64},{49,33},{64,... | collective-permute-start | bytes 1179656 | tf_op jit(solution)/shard_map/ppermute | solution.py:31
  61.8 0.6 collective-permute-start.13
  62.5 3.5 %collective-permute-start.14 = (bf16[2,2,128,384]{3,2,1,0:T(8,128)(2,1)S(1)}, bf16[2,2,128,384]{3,2,1,0:T(8,128)(2,1)S(1)}, u32[]{:S(2)}, u32[]{:S(2)}) collective-permute-start(bf16[2,2,128,384]{3,2,1,0:T(8,128)(2,1)S(1)} %get-tuple-element.44), channel_id=1, source_target_pairs={{0,8},{1,9},{16,24},{17,25},{32,40},{33,41},{48,56},{49,57},{64,72... | collective-permute-start | bytes 1179656 | tf_op jit(solution)/shard_map/ppermute | solution.py:31
  65.9 3.0 %collective-permute-done.16 = bf16[2,24,16,256]{3,2,1,0:T(8,128)(2,1)S(1)} collective-permute-done((bf16[2,24,16,256]{3,2,1,0:T(8,128)(2,1)S(1)}, bf16[2,24,16,256]{3,2,1,0:T(8,128)(2,1)S(1)}, u32[]{:S(2)}, u32[]{:S(2)}) %collective-permute-start.16) | collective-permute-done | bytes 393248 | tf_op jit(solution)/shard_map/ppermute | solution.py:31
  68.9 4.0 %collective-permute-done.17 = bf16[2,24,16,256]{3,2,1,0:T(8,128)(2,1)S(1)} collective-permute-done((bf16[2,24,16,256]{3,2,1,0:T(8,128)(2,1)S(1)}, bf16[2,24,16,256]{3,2,1,0:T(8,128)(2,1)S(1)}, u32[]{:S(2)}, u32[]{:S(2)}) %collective-permute-start.17) | collective-permute-done | bytes 393248 | tf_op jit(solution)/shard_map/ppermute | solution.py:31
  72.9 0.2 fusion.4
  73.2 0.3 collective-permute-start.19
  73.5 1.5 %collective-permute-start.20 = (bf16[2,24,16,256]{3,2,1,0:T(8,128)(2,1)S(1)}, bf16[2,24,16,256]{3,2,1,0:T(8,128)(2,1)S(1)}, u32[]{:S(2)}, u32[]{:S(2)}) collective-permute-start(bf16[2,24,16,256]{3,2,1,0:T(8,128)(2,1)S(1)} %get-tuple-element.49), channel_id=1, source_target_pairs={{0,112},{1,17},{16,0},{17,33},{32,16},{33,49},{48,32},{49,65},{64,... | collective-permute-start | bytes 1179656 | tf_op jit(solution)/shard_map/ppermute | solution.py:31
  74.9 7.0 %collective-permute-done.14 = bf16[2,2,128,384]{3,2,1,0:T(8,128)(2,1)S(1)} collective-permute-done((bf16[2,2,128,384]{3,2,1,0:T(8,128)(2,1)S(1)}, bf16[2,2,128,384]{3,2,1,0:T(8,128)(2,1)S(1)}, u32[]{:S(2)}, u32[]{:S(2)}) %collective-permute-start.14) | collective-permute-done | bytes 393248 | tf_op jit(solution)/shard_map/ppermute | solution.py:31
  81.9 0.4 collective-permute-done.15
  82.3 0.3 fusion.13
  82.6 1.6 %collective-permute-start.18 = (bf16[2,128,384]{2,1,0:T(8,128)(2,1)S(1)}, bf16[2,128,384]{2,1,0:T(8,128)(2,1)S(1)}, u32[]{:S(2)}, u32[]{:S(2)}) collective-permute-start(bf16[2,128,384]{2,1,0:T(8,128)(2,1)S(1)} %slice_bitcast_fusion.5), channel_id=1, source_target_pairs={{0,2},{1,3},{16,18},{17,19},{32,34},{33,35},{48,50},{49,51},{64,66... | collective-permute-start | bytes 589832 | tf_op jit(solution)/shard_map/ppermute | solution.py:31
  84.3 0.1 collective-permute-done.19
  84.3 0.8 collective-permute-done.20
  85.1 0.2 fusion.2
  85.4 3.4 %collective-permute-start.21 = (bf16[2,24,16,256]{3,2,1,0:T(8,128)(2,1)S(1)}, bf16[2,24,16,256]{3,2,1,0:T(8,128)(2,1)S(1)}, u32[]{:S(2)}, u32[]{:S(2)}) collective-permute-start(bf16[2,24,16,256]{3,2,1,0:T(8,128)(2,1)S(1)} %get-tuple-element.53), channel_id=1, source_target_pairs={{0,16},{1,113},{16,32},{17,1},{32,48},{33,17},{48,64},{49,33},{64,... | collective-permute-start | bytes 1179656 | tf_op jit(solution)/shard_map/ppermute | solution.py:31
  88.8 0.1 fusion.14
  88.8 0.7 slice_bitcast_fusion.7
  89.5 6.5 %collective-permute-done.21 = bf16[2,24,16,256]{3,2,1,0:T(8,128)(2,1)S(1)} collective-permute-done((bf16[2,24,16,256]{3,2,1,0:T(8,128)(2,1)S(1)}, bf16[2,24,16,256]{3,2,1,0:T(8,128)(2,1)S(1)}, u32[]{:S(2)}, u32[]{:S(2)}) %collective-permute-start.21) | collective-permute-done | bytes 393248 | tf_op jit(solution)/shard_map/ppermute | solution.py:31
  96.0 3.5 %collective-permute-done.22 = bf16[2,24,16,256]{3,2,1,0:T(8,128)(2,1)S(1)} collective-permute-done((bf16[2,24,16,256]{3,2,1,0:T(8,128)(2,1)S(1)}, bf16[2,24,16,256]{3,2,1,0:T(8,128)(2,1)S(1)}, u32[]{:S(2)}, u32[]{:S(2)}) %collective-permute-start.22) | collective-permute-done | bytes 393248 | tf_op jit(solution)/shard_map/ppermute | solution.py:31
  99.5 0.2 fusion.1
  99.7 0.8 fusion.16
  (14 shorter events, 0.1 us)
Async XLA Ops:
  1.6 6.9 %collective-permute-start.2 = (bf16[2,128,384]{2,1,0:T(8,128)(2,1)S(1)}, bf16[2,128,384]{2,1,0:T(8,128)(2,1)S(1)}, u32[]{:S(2)}, u32[]{:S(2)}) collective-permute-start(bf16[2,128,384]{2,1,0:T(8,128)(2,1)S(1)} %get-tuple-element.67), channel_id=1, source_target_pairs={{0,8},{1,3},{16,24},{17,19},{32,40},{33,35},{48,56},{49,51},{64,72... | collective-permute-start | bytes 589832 | tf_op jit(solution)/shard_map/gather/ppermute | solution.py:31
  5.4 6.0 %collective-permute-start.1 = (bf16[2,128,384]{2,1,0:T(8,128)(2,1)S(1)}, bf16[2,128,384]{2,1,0:T(8,128)(2,1)S(1)}, u32[]{:S(2)}, u32[]{:S(2)}) collective-permute-start(bf16[2,128,384]{2,1,0:T(8,128)(2,1)S(1)} %get-tuple-element.67), channel_id=1, source_target_pairs={{0,4},{1,129},{16,20},{17,145},{32,36},{33,161},{48,52},{49,177},{... | collective-permute-start | bytes 589832 | tf_op jit(solution)/shard_map/gather/ppermute | solution.py:31
  5.8 5.6 %collective-permute-start = (bf16[2,128,384]{2,1,0:T(8,128)(2,1)S(1)}, bf16[2,128,384]{2,1,0:T(8,128)(2,1)S(1)}, u32[]{:S(2)}, u32[]{:S(2)}) collective-permute-start(bf16[2,128,384]{2,1,0:T(8,128)(2,1)S(1)} %get-tuple-element.67), channel_id=1, source_target_pairs={{0,12},{1,131},{16,28},{17,147},{32,44},{33,163},{48,60},{49,179},... | collective-permute-start | bytes 589832 | tf_op jit(solution)/shard_map/gather/ppermute | solution.py:31
  11.6 12.8 %collective-permute-start.5 = (bf16[4,2,128,384]{3,2,1,0:T(8,128)(2,1)S(1)}, bf16[4,2,128,384]{3,2,1,0:T(8,128)(2,1)S(1)}, u32[]{:S(2)}, u32[]{:S(2)}) collective-permute-start(bf16[4,2,128,384]{3,2,1,0:T(8,128)(2,1)S(1)} %pad_maximum_fusion.refs_0_), channel_id=1, source_target_pairs={{0,2},{1,9},{16,18},{17,25},{32,34},{33,41},{48,50},{49,57},{64,66... | collective-permute-start | bytes 2359304 | tf_op jit(solution)/shard_map/gather/ppermute | solution.py:31
  14.3 18.6 %collective-permute-start.4 = (bf16[4,2,128,384]{3,2,1,0:T(8,128)(2,1)S(1)}, bf16[4,2,128,384]{3,2,1,0:T(8,128)(2,1)S(1)}, u32[]{:S(2)}, u32[]{:S(2)}) collective-permute-start(bf16[4,2,128,384]{3,2,1,0:T(8,128)(2,1)S(1)} %pad_maximum_fusion.refs_0_), channel_id=1, source_target_pairs={{0,130},{1,13},{16,146},{17,29},{32,162},{33,45},{48,178},{49,61},... | collective-permute-start | bytes 2359304 | tf_op jit(solution)/shard_map/gather/ppermute | solution.py:31
  15.1 20.5 %collective-permute-start.3 = (bf16[4,2,128,384]{3,2,1,0:T(8,128)(2,1)S(1)}, bf16[4,2,128,384]{3,2,1,0:T(8,128)(2,1)S(1)}, u32[]{:S(2)}, u32[]{:S(2)}) collective-permute-start(bf16[4,2,128,384]{3,2,1,0:T(8,128)(2,1)S(1)} %pad_maximum_fusion.refs_0_), channel_id=1, source_target_pairs={{0,128},{1,5},{16,144},{17,21},{32,160},{33,37},{48,176},{49,53},{... | collective-permute-start | bytes 2359304 | tf_op jit(solution)/shard_map/gather/ppermute | solution.py:31
  15.7 21.3 %collective-permute-start.6 = (bf16[4,2,128,384]{3,2,1,0:T(8,128)(2,1)S(1)}, bf16[4,2,128,384]{3,2,1,0:T(8,128)(2,1)S(1)}, u32[]{:S(2)}, u32[]{:S(2)}) collective-permute-start(bf16[4,2,128,384]{3,2,1,0:T(8,128)(2,1)S(1)} %pad_maximum_fusion.refs_0_), channel_id=1, source_target_pairs={{0,1},{1,0},{16,17},{17,16},{32,33},{33,32},{48,49},{49,48},{64,65... | collective-permute-start | bytes 2359304 | tf_op jit(solution)/shard_map/gather/ppermute | solution.py:31
  24.4 12.7 %collective-permute-start.9 = (bf16[4,2,128,384]{3,2,1,0:T(8,128)(2,1)S(1)}, bf16[4,2,128,384]{3,2,1,0:T(8,128)(2,1)S(1)}, u32[]{:S(2)}, u32[]{:S(2)}) collective-permute-start(bf16[4,2,128,384]{3,2,1,0:T(8,128)(2,1)S(1)} %collective-permute-done.5.refs_3_), channel_id=1, source_target_pairs={{0,1},{1,0},{16,17},{17,16},{32,33},{33,32},{48,49},{49,48},{64,65... | collective-permute-start | bytes 2359304 | tf_op jit(solution)/shard_map/gather/ppermute | solution.py:31
  32.9 4.7 %collective-permute-start.8 = (bf16[4,2,128,384]{3,2,1,0:T(8,128)(2,1)S(1)}, bf16[4,2,128,384]{3,2,1,0:T(8,128)(2,1)S(1)}, u32[]{:S(2)}, u32[]{:S(2)}) collective-permute-start(bf16[4,2,128,384]{3,2,1,0:T(8,128)(2,1)S(1)} %collective-permute-done.4.refs_2_), channel_id=1, source_target_pairs={{0,1},{1,0},{16,17},{17,16},{32,33},{33,32},{48,49},{49,48},{64,65... | collective-permute-start | bytes 2359304 | tf_op jit(solution)/shard_map/gather/ppermute | solution.py:31
  35.6 3.0 %collective-permute-start.7 = (bf16[4,2,128,384]{3,2,1,0:T(8,128)(2,1)S(1)}, bf16[4,2,128,384]{3,2,1,0:T(8,128)(2,1)S(1)}, u32[]{:S(2)}, u32[]{:S(2)}) collective-permute-start(bf16[4,2,128,384]{3,2,1,0:T(8,128)(2,1)S(1)} %collective-permute-done.3.refs_1_), channel_id=1, source_target_pairs={{0,1},{1,0},{16,17},{17,16},{32,33},{33,32},{48,49},{49,48},{64,65... | collective-permute-start | bytes 2359304 | tf_op jit(solution)/shard_map/gather/ppermute | solution.py:31
  47.4 10.9 %collective-permute-start.10 = (bf16[2,2,2,128,384]{4,3,2,1,0:T(8,128)(2,1)S(1)}, bf16[2,2,2,128,384]{4,3,2,1,0:T(8,128)(2,1)S(1)}, u32[]{:S(2)}, u32[]{:S(2)}) collective-permute-start(bf16[2,2,2,128,384]{4,3,2,1,0:T(8,128)(2,1)S(1)} %get-tuple-element.36), channel_id=1, source_target_pairs={{0,1},{1,0},{16,17},{17,16},{32,33},{33,32},{48,49},{49,48},{64,65... | collective-permute-start | bytes 2359304 | tf_op jit(solution)/shard_map/ppermute | solution.py:31
  47.9 10.3 %collective-permute-start.12 = (bf16[2,24,16,256]{3,2,1,0:T(8,128)(2,1)S(1)}, bf16[2,24,16,256]{3,2,1,0:T(8,128)(2,1)S(1)}, u32[]{:S(2)}, u32[]{:S(2)}) collective-permute-start(bf16[2,24,16,256]{3,2,1,0:T(8,128)(2,1)S(1)} %get-tuple-element.42), channel_id=1, source_target_pairs={{0,16},{1,113},{16,32},{17,1},{32,48},{33,17},{48,64},{49,33},{64,... | collective-permute-start | bytes 1179656 | tf_op jit(solution)/shard_map/ppermute | solution.py:31
  53.4 5.0 %collective-permute-start.11 = (bf16[2,2,2,128,384]{4,3,2,1,0:T(8,128)(2,1)S(1)}, bf16[2,2,2,128,384]{4,3,2,1,0:T(8,128)(2,1)S(1)}, u32[]{:S(2)}, u32[]{:S(2)}) collective-permute-start(bf16[2,2,2,128,384]{4,3,2,1,0:T(8,128)(2,1)S(1)} %get-tuple-element.38), channel_id=1, source_target_pairs={{0,1},{1,0},{16,17},{17,16},{32,33},{33,32},{48,49},{49,48},{64,65... | collective-permute-start | bytes 2359304 | tf_op jit(solution)/shard_map/ppermute | solution.py:31
  58.6 10.3 %collective-permute-start.16 = (bf16[2,24,16,256]{3,2,1,0:T(8,128)(2,1)S(1)}, bf16[2,24,16,256]{3,2,1,0:T(8,128)(2,1)S(1)}, u32[]{:S(2)}, u32[]{:S(2)}) collective-permute-start(bf16[2,24,16,256]{3,2,1,0:T(8,128)(2,1)S(1)} %fusion.6), channel_id=1, source_target_pairs={{0,16},{1,113},{16,32},{17,1},{32,48},{33,17},{48,64},{49,33},{64,... | collective-permute-start | bytes 1179656 | tf_op jit(solution)/shard_map/ppermute | solution.py:31
  61.8 11.1 %collective-permute-start.17 = (bf16[2,24,16,256]{3,2,1,0:T(8,128)(2,1)S(1)}, bf16[2,24,16,256]{3,2,1,0:T(8,128)(2,1)S(1)}, u32[]{:S(2)}, u32[]{:S(2)}) collective-permute-start(bf16[2,24,16,256]{3,2,1,0:T(8,128)(2,1)S(1)} %slice_bitcast_fusion.4), channel_id=1, source_target_pairs={{0,112},{1,17},{16,0},{17,33},{32,16},{33,49},{48,32},{49,65},{64,... | collective-permute-start | bytes 1179656 | tf_op jit(solution)/shard_map/ppermute | solution.py:31
  61.8 13.1 %collective-permute-start.13 = (bf16[2,2,128,384]{3,2,1,0:T(8,128)(2,1)S(1)}, bf16[2,2,128,384]{3,2,1,0:T(8,128)(2,1)S(1)}, u32[]{:S(2)}, u32[]{:S(2)}) collective-permute-start(bf16[2,2,128,384]{3,2,1,0:T(8,128)(2,1)S(1)} %get-tuple-element.43), channel_id=1, source_target_pairs={{0,4},{1,5},{16,20},{17,21},{32,36},{33,37},{48,52},{49,53},{64,68... | collective-permute-start | bytes 1179656 | tf_op jit(solution)/shard_map/ppermute | solution.py:31
  62.5 19.4 %collective-permute-start.14 = (bf16[2,2,128,384]{3,2,1,0:T(8,128)(2,1)S(1)}, bf16[2,2,128,384]{3,2,1,0:T(8,128)(2,1)S(1)}, u32[]{:S(2)}, u32[]{:S(2)}) collective-permute-start(bf16[2,2,128,384]{3,2,1,0:T(8,128)(2,1)S(1)} %get-tuple-element.44), channel_id=1, source_target_pairs={{0,8},{1,9},{16,24},{17,25},{32,40},{33,41},{48,56},{49,57},{64,72... | collective-permute-start | bytes 1179656 | tf_op jit(solution)/shard_map/ppermute | solution.py:31
  65.9 16.4 %collective-permute-start.15 = (bf16[2,2,128,384]{3,2,1,0:T(8,128)(2,1)S(1)}, bf16[2,2,128,384]{3,2,1,0:T(8,128)(2,1)S(1)}, u32[]{:S(2)}, u32[]{:S(2)}) collective-permute-start(bf16[2,2,128,384]{3,2,1,0:T(8,128)(2,1)S(1)} %fusion.7), channel_id=1, source_target_pairs={{0,12},{1,13},{16,28},{17,29},{32,44},{33,45},{48,60},{49,61},{64,... | collective-permute-start | bytes 1179656 | tf_op jit(solution)/shard_map/ppermute | solution.py:31
  73.2 11.1 %collective-permute-start.19 = (bf16[2,24,16,256]{3,2,1,0:T(8,128)(2,1)S(1)}, bf16[2,24,16,256]{3,2,1,0:T(8,128)(2,1)S(1)}, u32[]{:S(2)}, u32[]{:S(2)}) collective-permute-start(bf16[2,24,16,256]{3,2,1,0:T(8,128)(2,1)S(1)} %get-tuple-element.48), channel_id=1, source_target_pairs={{0,16},{1,113},{16,32},{17,1},{32,48},{33,17},{48,64},{49,33},{64,... | collective-permute-start | bytes 1179656 | tf_op jit(solution)/shard_map/ppermute | solution.py:31
  73.5 11.7 %collective-permute-start.20 = (bf16[2,24,16,256]{3,2,1,0:T(8,128)(2,1)S(1)}, bf16[2,24,16,256]{3,2,1,0:T(8,128)(2,1)S(1)}, u32[]{:S(2)}, u32[]{:S(2)}) collective-permute-start(bf16[2,24,16,256]{3,2,1,0:T(8,128)(2,1)S(1)} %get-tuple-element.49), channel_id=1, source_target_pairs={{0,112},{1,17},{16,0},{17,33},{32,16},{33,49},{48,32},{49,65},{64,... | collective-permute-start | bytes 1179656 | tf_op jit(solution)/shard_map/ppermute | solution.py:31
  82.6 6.2 %collective-permute-start.18 = (bf16[2,128,384]{2,1,0:T(8,128)(2,1)S(1)}, bf16[2,128,384]{2,1,0:T(8,128)(2,1)S(1)}, u32[]{:S(2)}, u32[]{:S(2)}) collective-permute-start(bf16[2,128,384]{2,1,0:T(8,128)(2,1)S(1)} %slice_bitcast_fusion.5), channel_id=1, source_target_pairs={{0,2},{1,3},{16,18},{17,19},{32,34},{33,35},{48,50},{49,51},{64,66... | collective-permute-start | bytes 589832 | tf_op jit(solution)/shard_map/ppermute | solution.py:31
  85.4 10.6 %collective-permute-start.21 = (bf16[2,24,16,256]{3,2,1,0:T(8,128)(2,1)S(1)}, bf16[2,24,16,256]{3,2,1,0:T(8,128)(2,1)S(1)}, u32[]{:S(2)}, u32[]{:S(2)}) collective-permute-start(bf16[2,24,16,256]{3,2,1,0:T(8,128)(2,1)S(1)} %get-tuple-element.53), channel_id=1, source_target_pairs={{0,16},{1,113},{16,32},{17,1},{32,48},{33,17},{48,64},{49,33},{64,... | collective-permute-start | bytes 1179656 | tf_op jit(solution)/shard_map/ppermute | solution.py:31
  88.8 10.7 %collective-permute-start.22 = (bf16[2,24,16,256]{3,2,1,0:T(8,128)(2,1)S(1)}, bf16[2,24,16,256]{3,2,1,0:T(8,128)(2,1)S(1)}, u32[]{:S(2)}, u32[]{:S(2)}) collective-permute-start(bf16[2,24,16,256]{3,2,1,0:T(8,128)(2,1)S(1)} %get-tuple-element.54), channel_id=1, source_target_pairs={{0,112},{1,17},{16,0},{17,33},{32,16},{33,49},{48,32},{49,65},{64,... | collective-permute-start | bytes 1179656 | tf_op jit(solution)/shard_map/ppermute | solution.py:31

commit v4 on v3

--- a/solution.py
+++ b/solution.py
@@ -75,7 +75,7 @@
     dy = (y - ((t & 2) + token_half)) & 3
     first = jnp.where(c == 0, dx, dy)
     second = jnp.where(c == 0, dy, dx)
-    return all_ref[kind, c ^ core, second, first, :, pl.ds(pl.multiple_of(lane, HALF), HALF)]
+    return all_ref[c ^ core, second, first, kind, :, pl.ds(pl.multiple_of(lane, HALF), HALF)]
 
 
 def gathered_block(all_ref, kind, b, x, y, core):
@@ -97,20 +97,15 @@
     ylo, z, x, yhi, core = place()
     y = yhi * 2 + ylo
 
-    def fetch(kind):
-        for slot in range(2):
-            for i, e in enumerate((0, 1, 3, 2)):
-                pltpu.make_async_copy(
-                    parts[4 * slot + i].at[:, kind], all_ref.at[kind, slot, e], sem.at[kind]
-                ).start()
+    for slot in range(2):
+        for i, e in enumerate((0, 1, 3, 2)):
+            pltpu.make_async_copy(parts[4 * slot + i], all_ref.at[slot, e], sem.at[0]).start()
 
     def await_all(ref, i):
         pltpu.make_async_copy(ref, ref, sem.at[i]).wait()
 
-    fetch(0)
     up_copy = pltpu.make_async_copy(up_hbm, up_ref, sem.at[2])
     up_copy.start()
-    fetch(1)
     down_copy = pltpu.make_async_copy(down_hbm, down_ref, sem.at[3])
     down_copy.start()
 
@@ -134,7 +129,7 @@
 
     acc_ref[...] = jnp.zeros_like(acc_ref)
     own = pl.ds(pl.multiple_of(ylo * HALF, HALF), HALF)
-    await_all(all_ref.at[0], 0)
+    await_all(all_ref, 0)
     up_copy.wait()
     for n in range(NH):
         acc = jnp.zeros((BLK, BLK), F32)
@@ -143,7 +138,6 @@
             acc += dot(tok, up_ref[n, k], 1, 0)
         pre_ref[n] = acc
         hid_ref[n] = (acc * jax.nn.sigmoid(acc)).astype(BF16)
-    await_all(all_ref.at[1], 1)
     down_copy.wait()
     for n in range(NH):
         hidden, my_hidden = hid_ref[n, :, own], hid_ref[n, own]
@@ -231,7 +225,7 @@
         [
             pltpu.VMEM((NH, BLK, BLK), BF16),
             pltpu.VMEM((32, HALF, WIDE), F32),
-            pltpu.VMEM((2, 2, 4, 4, HALF, WIDE), BF16),
+            pltpu.VMEM((2, 4, 4, 2, HALF, WIDE), BF16),
             pltpu.VMEM((NH, K, BLK, BLK), BF16),
             pltpu.VMEM((NH, K, BLK, BLK), BF16),
             pltpu.VMEM((NH, BLK, BLK), F32),
@@ -244,7 +238,8 @@
     ahead = permute(far, ahead_z)
     got_a, got_b = permute(give_a, other_core), permute(give_b, other_core)
     sums = [wide_sum(keep[dx], got) for dx, got in ((1, got_a[0]), (2, got_a[1]), (3, got_b[1]))]
-    *sums, ahead, back = tie((*sums, wide_sum(parts[3], ahead), parts[5]))
+    ahead, back = tie((wide_sum(parts[3], ahead), parts[5]))
+    *sums, _, _ = tie((*sums, ahead, back))
     ahead, back = permute(ahead, ahead_z), permute(back, back_z)
     sent = [permute(total, along_x(dx)) for dx, total in zip((1, 2, 3), sums)]
     ahead, back = tie((wide_sum(parts[2], ahead), wide_sum(parts[6], back)))

time: 101 us -> 101 us (level)
  transfers between devices with their start and end apart: 23 -> 23, of which waited for: 15 -> 14; matrix products, arithmetic and copies ran while one was open for 2% -> 3% of each run, Pallas kernels for 0% -> 0%
where the time goes in v4:
time: 101 us; the launch traced here: 100 us
  waiting for transfers between devices  45.1 us (45%)
  starting transfers between devices  41.3 us (41%)
  Pallas kernels  8.61 us (9%)
  other arithmetic  3.2 us (3%)
  local copies, waits for them, and re-layouts  1.51 us (1%)
    ppermute x23, waiting for transfers between devices, permute(): return lax.ppermute(value, AXES, pairs)  45.1 us
    ppermute x23, starting transfers between devices, permute(): return lax.ppermute(value, AXES, pairs)  41.3 us
    pallas_call x1, Pallas kernels, run(): pl.pallas_call(kernel, out_shape=tuple(out_shape), in_specs=in_specs, out...  8.61 us
  transfers between devices with their start and end apart: 23, of which 14 were waited for; matrix products, arithmetic and copies ran while one was open for 3% of the time, Pallas kernels for 0%

profile of v4, /device:TPU:1, one launch (start us, length us, event | category | flops | bytes accessed | tf_op | source)
XLA Modules:
  0.0 100.4 jit_solution(5625058727407366721)
XLA Ops:
  0.6 1.0 fusion.15
  1.6 3.8 %collective-permute-start.2 = (bf16[2,128,384]{2,1,0:T(8,128)(2,1)S(1)}, bf16[2,128,384]{2,1,0:T(8,128)(2,1)S(1)}, u32[]{:S(2)}, u32[]{:S(2)}) collective-permute-start(bf16[2,128,384]{2,1,0:T(8,128)(2,1)S(1)} %get-tuple-element.67), channel_id=1, source_target_pairs={{0,8},{1,3},{16,24},{17,19},{32,40},{33,35},{48,56},{49,51},{64,72... | collective-permute-start | bytes 589832 | tf_op jit(solution)/shard_map/gather/ppermute | solution.py:31
  5.4 0.4 collective-permute-start.1
  5.8 2.3 %collective-permute-start = (bf16[2,128,384]{2,1,0:T(8,128)(2,1)S(1)}, bf16[2,128,384]{2,1,0:T(8,128)(2,1)S(1)}, u32[]{:S(2)}, u32[]{:S(2)}) collective-permute-start(bf16[2,128,384]{2,1,0:T(8,128)(2,1)S(1)} %get-tuple-element.67), channel_id=1, source_target_pairs={{0,12},{1,131},{16,28},{17,147},{32,44},{33,163},{48,60},{49,179},... | collective-permute-start | bytes 589832 | tf_op jit(solution)/shard_map/gather/ppermute | solution.py:31
  8.1 0.4 collective-permute-done.2
  8.5 3.0 %collective-permute-done.1 = bf16[2,128,384]{2,1,0:T(8,128)(2,1)S(1)} collective-permute-done((bf16[2,128,384]{2,1,0:T(8,128)(2,1)S(1)}, bf16[2,128,384]{2,1,0:T(8,128)(2,1)S(1)}, u32[]{:S(2)}, u32[]{:S(2)}) %collective-permute-start.1) | collective-permute-done | bytes 196640 | tf_op jit(solution)/shard_map/gather/ppermute | solution.py:31
  11.5 0.1 pad_maximum_fusion.refs_0_
  11.6 2.7 %collective-permute-start.5 = (bf16[4,2,128,384]{3,2,1,0:T(8,128)(2,1)S(1)}, bf16[4,2,128,384]{3,2,1,0:T(8,128)(2,1)S(1)}, u32[]{:S(2)}, u32[]{:S(2)}) collective-permute-start(bf16[4,2,128,384]{3,2,1,0:T(8,128)(2,1)S(1)} %pad_maximum_fusion.refs_0_), channel_id=1, source_target_pairs={{0,2},{1,9},{16,18},{17,25},{32,34},{33,41},{48,50},{49,57},{64,66... | collective-permute-start | bytes 2359304 | tf_op jit(solution)/shard_map/gather/ppermute | solution.py:31
  14.3 0.9 collective-permute-start.4
  15.1 0.6 collective-permute-start.3
  15.7 2.8 %collective-permute-start.6 = (bf16[4,2,128,384]{3,2,1,0:T(8,128)(2,1)S(1)}, bf16[4,2,128,384]{3,2,1,0:T(8,128)(2,1)S(1)}, u32[]{:S(2)}, u32[]{:S(2)}) collective-permute-start(bf16[4,2,128,384]{3,2,1,0:T(8,128)(2,1)S(1)} %pad_maximum_fusion.refs_0_), channel_id=1, source_target_pairs={{0,1},{1,0},{16,17},{17,16},{32,33},{33,32},{48,49},{49,48},{64,65... | collective-permute-start | bytes 2359304 | tf_op jit(solution)/shard_map/gather/ppermute | solution.py:31
  18.5 5.8 %collective-permute-done.5.refs_3_ = bf16[4,2,128,384]{3,2,1,0:T(8,128)(2,1)S(1)} collective-permute-done((bf16[4,2,128,384]{3,2,1,0:T(8,128)(2,1)S(1)}, bf16[4,2,128,384]{3,2,1,0:T(8,128)(2,1)S(1)}, u32[]{:S(2)}, u32[]{:S(2)}) %collective-permute-start.5) | collective-permute-done | bytes 786464 | tf_op jit(solution)/shard_map/gather/ppermute | solution.py:31
  24.4 3.7 %collective-permute-start.9 = (bf16[4,2,128,384]{3,2,1,0:T(8,128)(2,1)S(1)}, bf16[4,2,128,384]{3,2,1,0:T(8,128)(2,1)S(1)}, u32[]{:S(2)}, u32[]{:S(2)}) collective-permute-start(bf16[4,2,128,384]{3,2,1,0:T(8,128)(2,1)S(1)} %collective-permute-done.5.refs_3_), channel_id=1, source_target_pairs={{0,1},{1,0},{16,17},{17,16},{32,33},{33,32},{48,49},{49,48},{64,65... | collective-permute-start | bytes 2359304 | tf_op jit(solution)/shard_map/gather/ppermute | solution.py:31
  28.0 4.8 %collective-permute-done.4.refs_2_ = bf16[4,2,128,384]{3,2,1,0:T(8,128)(2,1)S(1)} collective-permute-done((bf16[4,2,128,384]{3,2,1,0:T(8,128)(2,1)S(1)}, bf16[4,2,128,384]{3,2,1,0:T(8,128)(2,1)S(1)}, u32[]{:S(2)}, u32[]{:S(2)}) %collective-permute-start.4) | collective-permute-done | bytes 786464 | tf_op jit(solution)/shard_map/gather/ppermute | solution.py:31
  32.9 2.8 %collective-permute-start.8 = (bf16[4,2,128,384]{3,2,1,0:T(8,128)(2,1)S(1)}, bf16[4,2,128,384]{3,2,1,0:T(8,128)(2,1)S(1)}, u32[]{:S(2)}, u32[]{:S(2)}) collective-permute-start(bf16[4,2,128,384]{3,2,1,0:T(8,128)(2,1)S(1)} %collective-permute-done.4.refs_2_), channel_id=1, source_target_pairs={{0,1},{1,0},{16,17},{17,16},{32,33},{33,32},{48,49},{49,48},{64,65... | collective-permute-start | bytes 2359304 | tf_op jit(solution)/shard_map/gather/ppermute | solution.py:31
  35.6 0.7 collective-permute-start.7
  36.4 0.7 pad_add_fusion.index
  37.1 0.5 collective-permute-done.8.refs_6_
  37.5 1.1 %collective-permute-done.7.refs_5_ = bf16[4,2,128,384]{3,2,1,0:T(8,128)(2,1)S(1)} collective-permute-done((bf16[4,2,128,384]{3,2,1,0:T(8,128)(2,1)S(1)}, bf16[4,2,128,384]{3,2,1,0:T(8,128)(2,1)S(1)}, u32[]{:S(2)}, u32[]{:S(2)}) %collective-permute-start.7) | collective-permute-done | bytes 786464 | tf_op jit(solution)/shard_map/gather/ppermute | solution.py:31
  38.7 8.6 %grads.1 = (bf16[8,2,24,16,256]{4,3,2,1,0:T(8,128)(2,1)S(1)}, bf16[2,24,16,256]{3,2,1,0:T(8,128)(2,1)S(1)}, bf16[2,2,128,384]{3,2,1,0:T(8,128)(2,1)S(1)}, bf16[2...) custom-call(s32[2,4,6]{2,1,0:T(4,128)S(1)} %pad_add_fusion.index, ...), custom_call_target="tpu_custom_call" | custom-call | flops 3221225472 | bytes 12582912 | tf_op jit(solution)/shard_map/grads/pallas_call | solution.py:178
  47.3 0.5 collective-permute-start.10
  47.8 5.6 %collective-permute-start.12 = (bf16[2,24,16,256]{3,2,1,0:T(8,128)(2,1)S(1)}, bf16[2,24,16,256]{3,2,1,0:T(8,128)(2,1)S(1)}, u32[]{:S(2)}, u32[]{:S(2)}) collective-permute-start(bf16[2,24,16,256]{3,2,1,0:T(8,128)(2,1)S(1)} %get-tuple-element.42), channel_id=1, source_target_pairs={{0,16},{1,113},{16,32},{17,1},{32,48},{33,17},{48,64},{49,33},{64,... | collective-permute-start | bytes 1179656 | tf_op jit(solution)/shard_map/ppermute | solution.py:31
  53.4 4.7 %collective-permute-done.12 = bf16[2,24,16,256]{3,2,1,0:T(8,128)(2,1)S(1)} collective-permute-done((bf16[2,24,16,256]{3,2,1,0:T(8,128)(2,1)S(1)}, bf16[2,24,16,256]{3,2,1,0:T(8,128)(2,1)S(1)}, u32[]{:S(2)}, u32[]{:S(2)}) %collective-permute-start.12) | collective-permute-done | bytes 393248 | tf_op jit(solution)/shard_map/ppermute | solution.py:31
  58.0 0.1 fusion.6
  58.2 3.2 %collective-permute-start.16 = (bf16[2,24,16,256]{3,2,1,0:T(8,128)(2,1)S(1)}, bf16[2,24,16,256]{3,2,1,0:T(8,128)(2,1)S(1)}, u32[]{:S(2)}, u32[]{:S(2)}) collective-permute-start(bf16[2,24,16,256]{3,2,1,0:T(8,128)(2,1)S(1)} %fusion.6), channel_id=1, source_target_pairs={{0,16},{1,113},{16,32},{17,1},{32,48},{33,17},{48,64},{49,33},{64,... | collective-permute-start | bytes 1179656 | tf_op jit(solution)/shard_map/ppermute | solution.py:31
  61.4 0.1 fusion.7
  61.5 0.2 fusion.8
  61.7 0.7 collective-permute-start.13
  62.4 3.5 %collective-permute-start.14 = (bf16[2,2,128,384]{3,2,1,0:T(8,128)(2,1)S(1)}, bf16[2,2,128,384]{3,2,1,0:T(8,128)(2,1)S(1)}, u32[]{:S(2)}, u32[]{:S(2)}) collective-permute-start(bf16[2,2,128,384]{3,2,1,0:T(8,128)(2,1)S(1)} %get-tuple-element.46), channel_id=1, source_target_pairs={{0,8},{1,9},{16,24},{17,25},{32,40},{33,41},{48,56},{49,57},{64,72... | collective-permute-start | bytes 1179656 | tf_op jit(solution)/shard_map/ppermute | solution.py:31
  65.9 2.6 %collective-permute-done.16 = bf16[2,24,16,256]{3,2,1,0:T(8,128)(2,1)S(1)} collective-permute-done((bf16[2,24,16,256]{3,2,1,0:T(8,128)(2,1)S(1)}, bf16[2,24,16,256]{3,2,1,0:T(8,128)(2,1)S(1)}, u32[]{:S(2)}, u32[]{:S(2)}) %collective-permute-start.16) | collective-permute-done | bytes 393248 | tf_op jit(solution)/shard_map/ppermute | solution.py:31
  68.5 4.0 %collective-permute-done.17 = bf16[2,24,16,256]{3,2,1,0:T(8,128)(2,1)S(1)} collective-permute-done((bf16[2,24,16,256]{3,2,1,0:T(8,128)(2,1)S(1)}, bf16[2,24,16,256]{3,2,1,0:T(8,128)(2,1)S(1)}, u32[]{:S(2)}, u32[]{:S(2)}) %collective-permute-start.17) | collective-permute-done | bytes 393248 | tf_op jit(solution)/shard_map/ppermute | solution.py:31
  72.5 0.2 fusion.4
  72.7 0.3 collective-permute-start.19
  73.1 1.5 %collective-permute-start.20 = (bf16[2,24,16,256]{3,2,1,0:T(8,128)(2,1)S(1)}, bf16[2,24,16,256]{3,2,1,0:T(8,128)(2,1)S(1)}, u32[]{:S(2)}, u32[]{:S(2)}) collective-permute-start(bf16[2,24,16,256]{3,2,1,0:T(8,128)(2,1)S(1)} %get-tuple-element.49), channel_id=1, source_target_pairs={{0,112},{1,17},{16,0},{17,33},{32,16},{33,49},{48,32},{49,65},{64,... | collective-permute-start | bytes 1179656 | tf_op jit(solution)/shard_map/ppermute | solution.py:31
  74.5 7.4 %collective-permute-done.14 = bf16[2,2,128,384]{3,2,1,0:T(8,128)(2,1)S(1)} collective-permute-done((bf16[2,2,128,384]{3,2,1,0:T(8,128)(2,1)S(1)}, bf16[2,2,128,384]{3,2,1,0:T(8,128)(2,1)S(1)}, u32[]{:S(2)}, u32[]{:S(2)}) %collective-permute-start.14) | collective-permute-done | bytes 393248 | tf_op jit(solution)/shard_map/ppermute | solution.py:31
  81.9 0.5 collective-permute-done.15
  82.4 0.3 fusion.13
  82.7 1.7 %collective-permute-start.18 = (bf16[2,128,384]{2,1,0:T(8,128)(2,1)S(1)}, bf16[2,128,384]{2,1,0:T(8,128)(2,1)S(1)}, u32[]{:S(2)}, u32[]{:S(2)}) collective-permute-start(bf16[2,128,384]{2,1,0:T(8,128)(2,1)S(1)} %slice_bitcast_fusion.5), channel_id=1, source_target_pairs={{0,2},{1,3},{16,18},{17,19},{32,34},{33,35},{48,50},{49,51},{64,66... | collective-permute-start | bytes 589832 | tf_op jit(solution)/shard_map/ppermute | solution.py:31
  84.3 0.4 collective-permute-done.20
  84.7 0.2 fusion.2
  85.0 3.8 %collective-permute-start.21 = (bf16[2,24,16,256]{3,2,1,0:T(8,128)(2,1)S(1)}, bf16[2,24,16,256]{3,2,1,0:T(8,128)(2,1)S(1)}, u32[]{:S(2)}, u32[]{:S(2)}) collective-permute-start(bf16[2,24,16,256]{3,2,1,0:T(8,128)(2,1)S(1)} %get-tuple-element.53), channel_id=1, source_target_pairs={{0,16},{1,113},{16,32},{17,1},{32,48},{33,17},{48,64},{49,33},{64,... | collective-permute-start | bytes 1179656 | tf_op jit(solution)/shard_map/ppermute | solution.py:31
  88.8 0.0 collective-permute-done.18
  88.8 0.1 fusion.14
  88.8 0.7 slice_bitcast_fusion.7
  89.5 6.5 %collective-permute-done.21 = bf16[2,24,16,256]{3,2,1,0:T(8,128)(2,1)S(1)} collective-permute-done((bf16[2,24,16,256]{3,2,1,0:T(8,128)(2,1)S(1)}, bf16[2,24,16,256]{3,2,1,0:T(8,128)(2,1)S(1)}, u32[]{:S(2)}, u32[]{:S(2)}) %collective-permute-start.21) | collective-permute-done | bytes 393248 | tf_op jit(solution)/shard_map/ppermute | solution.py:31
  96.0 3.5 %collective-permute-done.22 = bf16[2,24,16,256]{3,2,1,0:T(8,128)(2,1)S(1)} collective-permute-done((bf16[2,24,16,256]{3,2,1,0:T(8,128)(2,1)S(1)}, bf16[2,24,16,256]{3,2,1,0:T(8,128)(2,1)S(1)}, u32[]{:S(2)}, u32[]{:S(2)}) %collective-permute-start.22) | collective-permute-done | bytes 393248 | tf_op jit(solution)/shard_map/ppermute | solution.py:31
  99.5 0.2 fusion.1
  99.6 0.8 fusion.16
  (14 shorter events, 0.1 us)
Async XLA Ops:
  1.6 6.9 %collective-permute-start.2 = (bf16[2,128,384]{2,1,0:T(8,128)(2,1)S(1)}, bf16[2,128,384]{2,1,0:T(8,128)(2,1)S(1)}, u32[]{:S(2)}, u32[]{:S(2)}) collective-permute-start(bf16[2,128,384]{2,1,0:T(8,128)(2,1)S(1)} %get-tuple-element.67), channel_id=1, source_target_pairs={{0,8},{1,3},{16,24},{17,19},{32,40},{33,35},{48,56},{49,51},{64,72... | collective-permute-start | bytes 589832 | tf_op jit(solution)/shard_map/gather/ppermute | solution.py:31
  5.4 6.0 %collective-permute-start.1 = (bf16[2,128,384]{2,1,0:T(8,128)(2,1)S(1)}, bf16[2,128,384]{2,1,0:T(8,128)(2,1)S(1)}, u32[]{:S(2)}, u32[]{:S(2)}) collective-permute-start(bf16[2,128,384]{2,1,0:T(8,128)(2,1)S(1)} %get-tuple-element.67), channel_id=1, source_target_pairs={{0,4},{1,129},{16,20},{17,145},{32,36},{33,161},{48,52},{49,177},{... | collective-permute-start | bytes 589832 | tf_op jit(solution)/shard_map/gather/ppermute | solution.py:31
  5.8 5.6 %collective-permute-start = (bf16[2,128,384]{2,1,0:T(8,128)(2,1)S(1)}, bf16[2,128,384]{2,1,0:T(8,128)(2,1)S(1)}, u32[]{:S(2)}, u32[]{:S(2)}) collective-permute-start(bf16[2,128,384]{2,1,0:T(8,128)(2,1)S(1)} %get-tuple-element.67), channel_id=1, source_target_pairs={{0,12},{1,131},{16,28},{17,147},{32,44},{33,163},{48,60},{49,179},... | collective-permute-start | bytes 589832 | tf_op jit(solution)/shard_map/gather/ppermute | solution.py:31
  11.6 12.8 %collective-permute-start.5 = (bf16[4,2,128,384]{3,2,1,0:T(8,128)(2,1)S(1)}, bf16[4,2,128,384]{3,2,1,0:T(8,128)(2,1)S(1)}, u32[]{:S(2)}, u32[]{:S(2)}) collective-permute-start(bf16[4,2,128,384]{3,2,1,0:T(8,128)(2,1)S(1)} %pad_maximum_fusion.refs_0_), channel_id=1, source_target_pairs={{0,2},{1,9},{16,18},{17,25},{32,34},{33,41},{48,50},{49,57},{64,66... | collective-permute-start | bytes 2359304 | tf_op jit(solution)/shard_map/gather/ppermute | solution.py:31
  14.3 18.6 %collective-permute-start.4 = (bf16[4,2,128,384]{3,2,1,0:T(8,128)(2,1)S(1)}, bf16[4,2,128,384]{3,2,1,0:T(8,128)(2,1)S(1)}, u32[]{:S(2)}, u32[]{:S(2)}) collective-permute-start(bf16[4,2,128,384]{3,2,1,0:T(8,128)(2,1)S(1)} %pad_maximum_fusion.refs_0_), channel_id=1, source_target_pairs={{0,130},{1,13},{16,146},{17,29},{32,162},{33,45},{48,178},{49,61},... | collective-permute-start | bytes 2359304 | tf_op jit(solution)/shard_map/gather/ppermute | solution.py:31
  15.1 20.5 %collective-permute-start.3 = (bf16[4,2,128,384]{3,2,1,0:T(8,128)(2,1)S(1)}, bf16[4,2,128,384]{3,2,1,0:T(8,128)(2,1)S(1)}, u32[]{:S(2)}, u32[]{:S(2)}) collective-permute-start(bf16[4,2,128,384]{3,2,1,0:T(8,128)(2,1)S(1)} %pad_maximum_fusion.refs_0_), channel_id=1, source_target_pairs={{0,128},{1,5},{16,144},{17,21},{32,160},{33,37},{48,176},{49,53},{... | collective-permute-start | bytes 2359304 | tf_op jit(solution)/shard_map/gather/ppermute | solution.py:31
  15.7 21.3 %collective-permute-start.6 = (bf16[4,2,128,384]{3,2,1,0:T(8,128)(2,1)S(1)}, bf16[4,2,128,384]{3,2,1,0:T(8,128)(2,1)S(1)}, u32[]{:S(2)}, u32[]{:S(2)}) collective-permute-start(bf16[4,2,128,384]{3,2,1,0:T(8,128)(2,1)S(1)} %pad_maximum_fusion.refs_0_), channel_id=1, source_target_pairs={{0,1},{1,0},{16,17},{17,16},{32,33},{33,32},{48,49},{49,48},{64,65... | collective-permute-start | bytes 2359304 | tf_op jit(solution)/shard_map/gather/ppermute | solution.py:31
  24.4 12.7 %collective-permute-start.9 = (bf16[4,2,128,384]{3,2,1,0:T(8,128)(2,1)S(1)}, bf16[4,2,128,384]{3,2,1,0:T(8,128)(2,1)S(1)}, u32[]{:S(2)}, u32[]{:S(2)}) collective-permute-start(bf16[4,2,128,384]{3,2,1,0:T(8,128)(2,1)S(1)} %collective-permute-done.5.refs_3_), channel_id=1, source_target_pairs={{0,1},{1,0},{16,17},{17,16},{32,33},{33,32},{48,49},{49,48},{64,65... | collective-permute-start | bytes 2359304 | tf_op jit(solution)/shard_map/gather/ppermute | solution.py:31
  32.9 4.7 %collective-permute-start.8 = (bf16[4,2,128,384]{3,2,1,0:T(8,128)(2,1)S(1)}, bf16[4,2,128,384]{3,2,1,0:T(8,128)(2,1)S(1)}, u32[]{:S(2)}, u32[]{:S(2)}) collective-permute-start(bf16[4,2,128,384]{3,2,1,0:T(8,128)(2,1)S(1)} %collective-permute-done.4.refs_2_), channel_id=1, source_target_pairs={{0,1},{1,0},{16,17},{17,16},{32,33},{33,32},{48,49},{49,48},{64,65... | collective-permute-start | bytes 2359304 | tf_op jit(solution)/shard_map/gather/ppermute | solution.py:31
  35.6 3.0 %collective-permute-start.7 = (bf16[4,2,128,384]{3,2,1,0:T(8,128)(2,1)S(1)}, bf16[4,2,128,384]{3,2,1,0:T(8,128)(2,1)S(1)}, u32[]{:S(2)}, u32[]{:S(2)}) collective-permute-start(bf16[4,2,128,384]{3,2,1,0:T(8,128)(2,1)S(1)} %collective-permute-done.3.refs_1_), channel_id=1, source_target_pairs={{0,1},{1,0},{16,17},{17,16},{32,33},{33,32},{48,49},{49,48},{64,65... | collective-permute-start | bytes 2359304 | tf_op jit(solution)/shard_map/gather/ppermute | solution.py:31
  47.3 14.1 %collective-permute-start.10 = (bf16[2,2,2,128,384]{4,3,2,1,0:T(8,128)(2,1)S(1)}, bf16[2,2,2,128,384]{4,3,2,1,0:T(8,128)(2,1)S(1)}, u32[]{:S(2)}, u32[]{:S(2)}) collective-permute-start(bf16[2,2,2,128,384]{4,3,2,1,0:T(8,128)(2,1)S(1)} %get-tuple-element.36), channel_id=1, source_target_pairs={{0,1},{1,0},{16,17},{17,16},{32,33},{33,32},{48,49},{49,48},{64,65... | collective-permute-start | bytes 2359304 | tf_op jit(solution)/shard_map/ppermute | solution.py:31
  47.8 10.3 %collective-permute-start.12 = (bf16[2,24,16,256]{3,2,1,0:T(8,128)(2,1)S(1)}, bf16[2,24,16,256]{3,2,1,0:T(8,128)(2,1)S(1)}, u32[]{:S(2)}, u32[]{:S(2)}) collective-permute-start(bf16[2,24,16,256]{3,2,1,0:T(8,128)(2,1)S(1)} %get-tuple-element.42), channel_id=1, source_target_pairs={{0,16},{1,113},{16,32},{17,1},{32,48},{33,17},{48,64},{49,33},{64,... | collective-permute-start | bytes 1179656 | tf_op jit(solution)/shard_map/ppermute | solution.py:31
  53.3 8.1 %collective-permute-start.11 = (bf16[2,2,2,128,384]{4,3,2,1,0:T(8,128)(2,1)S(1)}, bf16[2,2,2,128,384]{4,3,2,1,0:T(8,128)(2,1)S(1)}, u32[]{:S(2)}, u32[]{:S(2)}) collective-permute-start(bf16[2,2,2,128,384]{4,3,2,1,0:T(8,128)(2,1)S(1)} %get-tuple-element.38), channel_id=1, source_target_pairs={{0,1},{1,0},{16,17},{17,16},{32,33},{33,32},{48,49},{49,48},{64,65... | collective-permute-start | bytes 2359304 | tf_op jit(solution)/shard_map/ppermute | solution.py:31
  58.2 10.3 %collective-permute-start.16 = (bf16[2,24,16,256]{3,2,1,0:T(8,128)(2,1)S(1)}, bf16[2,24,16,256]{3,2,1,0:T(8,128)(2,1)S(1)}, u32[]{:S(2)}, u32[]{:S(2)}) collective-permute-start(bf16[2,24,16,256]{3,2,1,0:T(8,128)(2,1)S(1)} %fusion.6), channel_id=1, source_target_pairs={{0,16},{1,113},{16,32},{17,1},{32,48},{33,17},{48,64},{49,33},{64,... | collective-permute-start | bytes 1179656 | tf_op jit(solution)/shard_map/ppermute | solution.py:31
  61.4 11.1 %collective-permute-start.17 = (bf16[2,24,16,256]{3,2,1,0:T(8,128)(2,1)S(1)}, bf16[2,24,16,256]{3,2,1,0:T(8,128)(2,1)S(1)}, u32[]{:S(2)}, u32[]{:S(2)}) collective-permute-start(bf16[2,24,16,256]{3,2,1,0:T(8,128)(2,1)S(1)} %slice_bitcast_fusion.4), channel_id=1, source_target_pairs={{0,112},{1,17},{16,0},{17,33},{32,16},{33,49},{48,32},{49,65},{64,... | collective-permute-start | bytes 1179656 | tf_op jit(solution)/shard_map/ppermute | solution.py:31
  61.7 12.8 %collective-permute-start.13 = (bf16[2,2,128,384]{3,2,1,0:T(8,128)(2,1)S(1)}, bf16[2,2,128,384]{3,2,1,0:T(8,128)(2,1)S(1)}, u32[]{:S(2)}, u32[]{:S(2)}) collective-permute-start(bf16[2,2,128,384]{3,2,1,0:T(8,128)(2,1)S(1)} %get-tuple-element.45), channel_id=1, source_target_pairs={{0,4},{1,5},{16,20},{17,21},{32,36},{33,37},{48,52},{49,53},{64,68... | collective-permute-start | bytes 1179656 | tf_op jit(solution)/shard_map/ppermute | solution.py:31
  62.4 19.5 %collective-permute-start.14 = (bf16[2,2,128,384]{3,2,1,0:T(8,128)(2,1)S(1)}, bf16[2,2,128,384]{3,2,1,0:T(8,128)(2,1)S(1)}, u32[]{:S(2)}, u32[]{:S(2)}) collective-permute-start(bf16[2,2,128,384]{3,2,1,0:T(8,128)(2,1)S(1)} %get-tuple-element.46), channel_id=1, source_target_pairs={{0,8},{1,9},{16,24},{17,25},{32,40},{33,41},{48,56},{49,57},{64,72... | collective-permute-start | bytes 1179656 | tf_op jit(solution)/shard_map/ppermute | solution.py:31
  65.9 16.5 %collective-permute-start.15 = (bf16[2,2,128,384]{3,2,1,0:T(8,128)(2,1)S(1)}, bf16[2,2,128,384]{3,2,1,0:T(8,128)(2,1)S(1)}, u32[]{:S(2)}, u32[]{:S(2)}) collective-permute-start(bf16[2,2,128,384]{3,2,1,0:T(8,128)(2,1)S(1)} %fusion.7), channel_id=1, source_target_pairs={{0,12},{1,13},{16,28},{17,29},{32,44},{33,45},{48,60},{49,61},{64,... | collective-permute-start | bytes 1179656 | tf_op jit(solution)/shard_map/ppermute | solution.py:31
  72.7 11.6 %collective-permute-start.19 = (bf16[2,24,16,256]{3,2,1,0:T(8,128)(2,1)S(1)}, bf16[2,24,16,256]{3,2,1,0:T(8,128)(2,1)S(1)}, u32[]{:S(2)}, u32[]{:S(2)}) collective-permute-start(bf16[2,24,16,256]{3,2,1,0:T(8,128)(2,1)S(1)} %get-tuple-element.48), channel_id=1, source_target_pairs={{0,16},{1,113},{16,32},{17,1},{32,48},{33,17},{48,64},{49,33},{64,... | collective-permute-start | bytes 1179656 | tf_op jit(solution)/shard_map/ppermute | solution.py:31
  73.1 11.7 %collective-permute-start.20 = (bf16[2,24,16,256]{3,2,1,0:T(8,128)(2,1)S(1)}, bf16[2,24,16,256]{3,2,1,0:T(8,128)(2,1)S(1)}, u32[]{:S(2)}, u32[]{:S(2)}) collective-permute-start(bf16[2,24,16,256]{3,2,1,0:T(8,128)(2,1)S(1)} %get-tuple-element.49), channel_id=1, source_target_pairs={{0,112},{1,17},{16,0},{17,33},{32,16},{33,49},{48,32},{49,65},{64,... | collective-permute-start | bytes 1179656 | tf_op jit(solution)/shard_map/ppermute | solution.py:31
  82.7 6.1 %collective-permute-start.18 = (bf16[2,128,384]{2,1,0:T(8,128)(2,1)S(1)}, bf16[2,128,384]{2,1,0:T(8,128)(2,1)S(1)}, u32[]{:S(2)}, u32[]{:S(2)}) collective-permute-start(bf16[2,128,384]{2,1,0:T(8,128)(2,1)S(1)} %slice_bitcast_fusion.5), channel_id=1, source_target_pairs={{0,2},{1,3},{16,18},{17,19},{32,34},{33,35},{48,50},{49,51},{64,66... | collective-permute-start | bytes 589832 | tf_op jit(solution)/shard_map/ppermute | solution.py:31
  85.0 11.1 %collective-permute-start.21 = (bf16[2,24,16,256]{3,2,1,0:T(8,128)(2,1)S(1)}, bf16[2,24,16,256]{3,2,1,0:T(8,128)(2,1)S(1)}, u32[]{:S(2)}, u32[]{:S(2)}) collective-permute-start(bf16[2,24,16,256]{3,2,1,0:T(8,128)(2,1)S(1)} %get-tuple-element.53), channel_id=1, source_target_pairs={{0,16},{1,113},{16,32},{17,1},{32,48},{33,17},{48,64},{49,33},{64,... | collective-permute-start | bytes 1179656 | tf_op jit(solution)/shard_map/ppermute | solution.py:31
  88.8 10.7 %collective-permute-start.22 = (bf16[2,24,16,256]{3,2,1,0:T(8,128)(2,1)S(1)}, bf16[2,24,16,256]{3,2,1,0:T(8,128)(2,1)S(1)}, u32[]{:S(2)}, u32[]{:S(2)}) collective-permute-start(bf16[2,24,16,256]{3,2,1,0:T(8,128)(2,1)S(1)} %get-tuple-element.54), channel_id=1, source_target_pairs={{0,112},{1,17},{16,0},{17,33},{32,16},{33,49},{48,32},{49,65},{64,... | collective-permute-start | bytes 1179656 | tf_op jit(solution)/shard_map/ppermute | solution.py:31
